TPU v7x, 256 devices: a whole 4x4x8 slice. The times are simulated.
256 devices in a mesh: ctx: 8 (over x_lo, y), fsdp: 16 (over z, x_hi), dp: 2 (over core).
Axes of the slice: x: 4 (x_hi: 2, x_lo: 2; x = x_hi * 2 + x_lo), y: 4, z: 8, core: 2. Of those that a mesh axis runs over, the one named last changes fastest.
Arguments:
- frames: bfloat16 [32, 1024, 1536], P(('dp', 'fsdp'), 'ctx'), parts along dimension 0, may hold values from -6 to 6
- lengths: int32 [32], P(('dp', 'fsdp')), parts along dimension 0, may hold values from 256 to 1024, as said below
- w_qkv: bfloat16 [1536, 2304], P('fsdp'), may hold values from -2.5 to 2.5
- w_out: bfloat16 [768, 1536], P('fsdp'), may hold values from -0.21875 to 0.21875
- w_glu: bfloat16 [1536, 3072], P('fsdp'), may hold values from -0.15625 to 0.15625
- depth_kernel: bfloat16 [31, 1536], replicated, may hold values from -1 to 1
- w_conv_out: bfloat16 [1536, 1536], P('fsdp'), may hold values from -0.15625 to 0.15625
Outputs:
- block_out: bfloat16 [32, 1024, 1536], P(('dp', 'fsdp'), 'ctx'), parts along dimension 0
There are 2 independent parts, one for each index of `dp`. A program takes and returns all parts, laid end to end along the dimension named above; an argument that names none is the same for every part. Nothing has to cross between parts.
Inputs may be any that keep to these rules, and one draw needn't show every extreme that they name: `lengths`: valid frames of each recording; in every draw some recording has all 1024 frames valid.
All inputs are finite; a program needn't handle non-finite values.
Results may differ from a plain program's by a relative error of at most 0.012.
Values may be sent and summed in bfloat16 or wider, within the bound.
No kernel may reach another device: no remote copies, remote signals or barrier semaphores. Data moves between devices by JAX's collectives and lax.ppermute only.
A program may use at most 64 MiB of HBM per device.

v0:
```python
import jax
import jax.numpy as jnp
from jax import lax
from jax.sharding import PartitionSpec as P

HEADS = 8
DH = 96
TAPS = 31


masked_score = -1e30


def with_halo(array, sides, width):
    for axis, dim in sides:
        size, length = (lax.axis_size(axis), array.shape[dim])
        up = [(i, (i + 1) % size) for i in range(size - 1)]
        down = [(j, i) for i, j in up]
        last = lax.slice_in_dim(array, length - width, length, axis=dim)
        leading = lax.slice_in_dim(array, 0, width, axis=dim)
        before = lax.ppermute(last, axis, up)
        after = lax.ppermute(leading, axis, down)
        array = jnp.concatenate([before, array, after], axis=dim)
    return array


def layer_norm(values):
    middle = jnp.mean(values, axis=-1, keepdims=True)
    spread = jnp.mean((values - middle) ** 2, axis=-1, keepdims=True)
    return (values - middle) * lax.rsqrt(spread + 1e-05)


def fold_into(operand, shard_piece):
    return jnp.dot(operand, shard_piece, preferred_element_type=jnp.float32)


def glu_product(operand, w_glu):
    return fold_into(operand, lax.all_gather(w_glu, "fsdp", axis=0, tiled=True))


def per_device(frames, lengths, w_qkv, w_out, w_glu, depth_kernel, w_conv_out):
    frame_rows = frames[0]
    length = lengths[0]
    rows = frame_rows.shape[0]
    width = w_qkv.shape[1] // 3
    model_width = frame_rows.shape[1]
    half_taps = TAPS // 2
    first_row = lax.axis_index("ctx") * rows
    positions = first_row + jnp.arange(rows)
    normed = layer_norm(frame_rows.astype(jnp.float32)).astype(jnp.bfloat16)
    qkv = fold_into(normed, lax.all_gather(w_qkv, "fsdp", axis=0, tiled=True)).astype(jnp.bfloat16)
    query_rows = qkv[:, :width].reshape(rows, HEADS, DH)
    key_rows = qkv[:, width : 2 * width].reshape(rows, HEADS, DH)
    value_rows = qkv[:, 2 * width :].reshape(rows, HEADS, DH)
    row_max = jnp.full((HEADS, rows), masked_score, jnp.float32)
    piece_keys = lax.all_gather(key_rows, "ctx", axis=0, tiled=True)
    piece_values = lax.all_gather(value_rows, "ctx", axis=0, tiled=True)
    key_pos = jnp.arange(piece_keys.shape[0])
    scores = jnp.einsum(
        "qhd,khd->hqk", query_rows, piece_keys, preferred_element_type=jnp.float32
    ) * DH ** (-0.5)
    scores = jnp.where((key_pos < length)[None, None, :], scores, masked_score)
    new_max = jnp.maximum(row_max, jnp.max(scores, axis=-1))
    exp_scores = jnp.exp(scores - new_max[:, :, None])
    new_total = jnp.sum(exp_scores, axis=-1)
    added = jnp.einsum(
        "hqk,khd->qhd",
        exp_scores.astype(jnp.bfloat16),
        piece_values,
        preferred_element_type=jnp.float32,
    )
    attended = (
        (added / jnp.transpose(new_total)[:, :, None]).astype(jnp.bfloat16).reshape(rows, width)
    )
    projected = fold_into(attended, lax.all_gather(w_out, "fsdp", axis=0, tiled=True))
    mixed = (frame_rows.astype(jnp.float32) + projected).astype(jnp.bfloat16)
    renormed = layer_norm(mixed.astype(jnp.float32)).astype(jnp.bfloat16)
    glu_in = glu_product(renormed, w_glu)
    gated = glu_in[:, :model_width] * jax.nn.sigmoid(glu_in[:, model_width:])
    gated = jnp.where((positions < length)[:, None], gated, jnp.float32(0.0)).astype(jnp.bfloat16)
    extended = with_halo(gated, (("ctx", 0),), half_taps)
    extended_float = extended.astype(jnp.float32)
    kernel = depth_kernel.astype(jnp.float32)
    conv_sum = jnp.zeros((rows, model_width), jnp.float32)
    for tap_index in range(TAPS):
        conv_sum = (
            conv_sum + kernel[tap_index][None, :] * extended_float[tap_index : tap_index + rows]
        )
    activated = jax.nn.silu(layer_norm(conv_sum)).astype(jnp.bfloat16)
    conv_projected = fold_into(activated, lax.all_gather(w_conv_out, "fsdp", axis=0, tiled=True))
    result = mixed.astype(jnp.float32) + conv_projected
    return result.astype(jnp.bfloat16)[None]


def solution(mesh):
    in_specs = (
        P(("dp", "fsdp"), "ctx", None),
        P(("dp", "fsdp")),
        P("fsdp", None),
        P("fsdp", None),
        P("fsdp", None),
        P(),
        P("fsdp", None),
    )
    out_specs = P(("dp", "fsdp"), "ctx", None)
    return jax.shard_map(
        per_device, mesh=mesh, in_specs=in_specs, out_specs=out_specs, check_vma=False
    )
```

profile of v0, /device:TPU:3, one launch (start us, length us, event | category | flops | bytes accessed | tf_op | source)
XLA Modules:
  0.0 575.5 jit_solution(13934166087534878710)
XLA Ops:
  6.5 0.0 all-gather.7.cloned.1.call-start
  6.5 0.7 all-gather.7.cloned.1.call-update
  7.3 0.0 all-gather.11.cloned.1.call-start
  7.3 1.1 convert_reduce_fusion
  8.4 1.2 fusion.25
  9.7 0.0 copy-start.2
  9.7 124.9 %all-gather.7.cloned.1.call-done = bf16[1536,2304]{1,0:T(8,128)(2,1)} async-done(((bf16[96,2304]{1,0:T(8,128)(2,1)}), bf16[1536,2304]{1,0:T(8,128)(2,1)}) %all-gather.7.cloned.1.call-update) | async-done | bytes 7077904 | tf_op jit(solution)/shard_map/all_gather | solution.py:51
  134.6 4.3 convolution_convert_fusion
  139.0 0.8 copy.13
  139.8 0.0 all-gather.11.cloned.1.call-update
  139.8 0.0 all-gather.9.cloned.1.call-start
  139.9 0.8 copy.11
  140.7 0.0 all-gather.9.cloned.1.call-update
  140.7 0.0 all-gather.13.cloned.1.call-start
  140.8 0.5 all-gather.13.cloned.1.call-update
  141.3 0.0 all-gather.15.cloned.1.call-start
  141.3 0.5 all-gather.15.cloned.1.call-update
  141.9 0.0 all-gather.17.cloned.1.call-start
  141.9 0.5 all-gather.17.cloned.1.call-update
  143.1 0.0 copy-done.2
  143.2 0.3 slice_reduce_fusion.30
  143.5 0.2 copy.12
  143.7 33.9 %all-gather.11.cloned.1.call-done = bf16[1024,8,96]{0,2,1:T(8,128)(2,1)} async-done(((bf16[128,8,96]{0,2,1:T(8,128)(2,1)}), bf16[1024,8,96]{0,2,1:T(8,128)(2,1)}) %all-gather.11.cloned.1.call-update) | async-done | bytes 1572880 | tf_op jit(solution)/shard_map/all_gather | solution.py:56
  177.5 2.3 fusion
  179.9 0.0 copy-start
  179.9 1.9 copy-done
  181.8 1.0 fusion.1
  182.9 41.4 %all-gather.9.cloned.1.call-done = bf16[1024,8,96]{0,2,1:T(8,128)(2,1)} async-done(((bf16[128,8,96]{0,2,1:T(8,128)(2,1)}), bf16[1024,8,96]{0,2,1:T(8,128)(2,1)}) %all-gather.9.cloned.1.call-update) | async-done | bytes 1572880 | tf_op jit(solution)/shard_map/all_gather | solution.py:57
  224.3 0.0 copy-start.1
  224.3 3.8 fusion.19
  228.2 87.3 %all-gather.13.cloned.1.call-done = bf16[768,1536]{1,0:T(8,128)(2,1)} async-done(((bf16[48,1536]{1,0:T(8,128)(2,1)}), bf16[768,1536]{1,0:T(8,128)(2,1)}) %all-gather.13.cloned.1.call-update) | async-done | bytes 2359312 | tf_op jit(solution)/shard_map/all_gather | solution.py:75
  315.5 0.0 copy-done.1
  315.5 2.2 fusion.79
  317.7 0.2 multiply_reduce_fusion.1
  318.0 146.3 %all-gather.15.cloned.1.call-done = bf16[1536,3072]{1,0:T(8,128)(2,1)} async-done(((bf16[96,3072]{1,0:T(8,128)(2,1)}), bf16[1536,3072]{1,0:T(8,128)(2,1)}) %all-gather.15.cloned.1.call-update) | async-done | bytes 9437200 | tf_op jit(solution)/shard_map/all_gather | solution.py:38
  464.3 5.2 fusion.63
  469.4 0.2 fusion.62
  469.7 3.1 collective-permute-start
  472.8 4.3 collective-permute-start.1
  477.1 0.2 slice_reduce_fusion.29
  477.3 0.0 collective-permute-done
  477.3 0.9 collective-permute-done.1
  478.2 0.1 maximum_convert_fusion
  478.4 3.2 fusion.75
  481.6 0.2 multiply_reduce_fusion
  481.9 82.8 %all-gather.17.cloned.1.call-done = bf16[1536,1536]{1,0:T(8,128)(2,1)} async-done(((bf16[96,1536]{1,0:T(8,128)(2,1)}), bf16[1536,1536]{1,0:T(8,128)(2,1)}) %all-gather.17.cloned.1.call-update) | async-done | bytes 4718608 | tf_op jit(solution)/shard_map/all_gather | solution.py:90
  564.7 4.0 fusion.6
  (12 shorter events, 0.1 us)
Async XLA Ops:
  6.5 128.1 %all-gather.7.cloned.1.call-start = ((), (), s32[]{:S(2)}) async-start(), calls=%async_computation | async-start | bytes 7520256 | tf_op jit(solution)/shard_map/all_gather | solution.py:51
  7.3 170.3 %all-gather.11.cloned.1.call-start = ((), (), s32[]{:S(2)}) async-start(), calls=%async_computation.2 | async-start | bytes 1769472 | tf_op jit(solution)/shard_map/all_gather | solution.py:56
  9.7 133.4 %copy-start.2 = (bf16[31,1536]{1,0:T(8,128)(2,1)S(1)}, bf16[31,1536]{1,0:T(8,128)(2,1)}, u32[]{:S(2)}) copy-start(bf16[31,1536]{1,0:T(8,128)(2,1)} %param.12) | copy-start | bytes 285700
  139.8 84.5 %all-gather.9.cloned.1.call-start = ((), (), s32[]{:S(2)}) async-start(), calls=%async_computation.1 | async-start | bytes 1769472 | tf_op jit(solution)/shard_map/all_gather | solution.py:57
  140.7 174.7 %all-gather.13.cloned.1.call-start = ((), (), s32[]{:S(2)}) async-start(), calls=%async_computation.3 | async-start | bytes 2506752 | tf_op jit(solution)/shard_map/all_gather | solution.py:75
  141.3 323.0 %all-gather.15.cloned.1.call-start = ((), (), s32[]{:S(2)}) async-start(), calls=%async_computation.4 | async-start | bytes 10027008 | tf_op jit(solution)/shard_map/all_gather | solution.py:38
  141.9 422.8 %all-gather.17.cloned.1.call-start = ((), (), s32[]{:S(2)}) async-start(), calls=%async_computation.5 | async-start | bytes 5013504 | tf_op jit(solution)/shard_map/all_gather | solution.py:90
  179.9 1.9 copy-start
  224.3 91.2 %copy-start.1 = (bf16[1,128,1536]{2,1,0:T(8,128)(2,1)S(1)}, bf16[1,128,1536]{2,1,0:T(8,128)(2,1)}, u32[]{:S(2)}) copy-start(bf16[1,128,1536]{2,1,0:T(8,128)(2,1)} %param.7) | copy-start | bytes 1179652
  469.7 7.6 %collective-permute-start = (bf16[15,1536]{1,0:T(8,128)(2,1)S(1)}, bf16[15,1536]{1,0:T(8,128)(2,1)S(1)}, u32[]{:S(2)}, u32[]{:S(2)}) collective-permute-start(bf16[15,1536]{1,0:T(8,128)(2,1)S(1)} %get-tuple-element.41), channel_id=1, source_target_pairs={{0,32},{32,64},{64,96},{96,128},{128,160},{160,192},{192,224},{1,3... | collective-permute-start | bytes 138248 | tf_op jit(solution)/shard_map/ppermute | solution.py:21
  472.8 5.4 collective-permute-start.1
Sparse Core Ops, SparseCore 0:
  9.9 124.6 all-gather.6
  140.0 37.5 all-gather.10
  179.3 45.0 all-gather.8
  226.7 88.6 all-gather.12
  317.9 146.3 all-gather.14
  466.7 97.9 all-gather.16
where the time goes:
time: 580 us; the launch traced here: 576 us
  waiting for transfers between devices  520 us (90%)
  matrix products  21.9 us (4%)
  between operations  14.3 us (2%)
  starting transfers between devices  7.59 us (1%)
  other arithmetic  7.55 us (1%)
    all_gather x1, waiting for transfers between devices, glu_product(): return fold_into(operand, lax.all_gather(w_glu, 'fsdp', axis=0, tiled=True))  146 us
    all_gather x1, waiting for transfers between devices, per_device(): lax.all_gather(w_qkv, 'fsdp', axis=0, tiled=True)  125 us
    all_gather x1, waiting for transfers between devices, per_device(): lax.all_gather(w_out, 'fsdp', axis=0, tiled=True)  87.3 us
    all_gather x1, waiting for transfers between devices, per_device(): lax.all_gather(w_conv_out, 'fsdp', axis=0, tiled=True)  82.8 us
    all_gather x1, waiting for transfers between devices, per_device(): piece_values = lax.all_gather(value_rows, 'ctx', axis=0, tiled=True)  41.4 us
    all_gather x1, waiting for transfers between devices, per_device(): piece_keys = lax.all_gather(key_rows, 'ctx', axis=0, tiled=True)  33.9 us
    dot_general x4, matrix products, fold_into(): return jnp.dot(operand, shard_piece, preferred_element_type=jnp.float32)  15.7 us
  transfers between devices with their start and end apart: 8, of which 7 were waited for; matrix products, arithmetic and copies ran while one was open for 4% of the time, Pallas kernels for 0%

commit v1 on v0

v1 whole, which is shorter than its diff:
```python
import numpy as np
import jax
import jax.numpy as jnp
from jax import lax
from jax.experimental import pallas as pl
from jax.experimental.pallas import tpu as pltpu
from jax.sharding import PartitionSpec as P

HEADS = 8
DH = 96
TAPS = 31
D = 1536
ROWS = 128
SEQ = 1024
LANES = 128
HALO = 16
WIDE = ROWS + 2 * HALO
masked_score = -1e30

AXES = ("ctx", "fsdp", "dp")
SHAPE = (2, 4, 8, 2, 2)
F32 = jnp.float32
BF16 = jnp.bfloat16


def pairs(move):
    out = []
    for i in range(256):
        c = [int(v) for v in np.unravel_index(i, SHAPE)]
        out.append((i, int(np.ravel_multi_index(move(*c), SHAPE))))
    return out


def xor_y(k):
    return pairs(lambda a, y, z, h, c: (a, y ^ k, z, h, c))


def xor_x(k):
    return pairs(lambda a, y, z, h, c: (a ^ (k & 1), y, z, h ^ (k >> 1), c))


def shift_z(k):
    return pairs(lambda a, y, z, h, c: (a, y, (z + k) % 8, h, c))


SWAP_CORE = pairs(lambda a, y, z, h, c: (a, y, z, h, 1 - c))
SWAP_H = pairs(lambda a, y, z, h, c: (a, y, z, 1 - h, c))

def send(value, moves):
    return lax.ppermute(value, AXES, moves)


def params(mib=60):
    return pltpu.CompilerParams(vmem_limit_bytes=mib * 2**20)


def cost(flops):
    return pl.CostEstimate(flops=flops, bytes_accessed=2**20, transcendentals=0)


def after(value, *others):
    return lax.optimization_barrier((value,) + others)[0]


def whereabouts():
    ctx, fsdp = lax.axis_index("ctx"), lax.axis_index("fsdp")
    return ctx, ctx & 3, ctx >> 2, fsdp >> 1, fsdp & 1, lax.axis_index("dp")


VM = pl.BlockSpec(memory_space=pltpu.VMEM)
SM = pl.BlockSpec(memory_space=pltpu.SMEM)
ANY = pl.BlockSpec(memory_space=pl.ANY)


def norm_rows(values):
    middle = jnp.mean(values, axis=-1, keepdims=True)
    apart = values - middle
    spread = jnp.mean(apart * apart, axis=-1, keepdims=True)
    return apart * lax.rsqrt(spread + 1e-05)


def columns(block, count=1):
    return pl.ds(pl.multiple_of(block * LANES, LANES), count * LANES)


def run_copies(copies, sems):
    made = [pltpu.make_async_copy(src, dst, sems.at[i]) for i, (src, dst) in enumerate(copies)]
    for copy in made:
        copy.start()

    def wait():
        for copy in made:
            copy.wait()

    return wait


BETA, GAMMA = 480, 528
NEAR = BETA // 2 + 288


def pack_kernel(x, w_qkv, w_out, w_glu, w_conv, beta, gam, normed, held, rows, sems):
    ctx, y, a, _, _, core = whereabouts()
    glu, conv = core * 12, core * 6
    copies = [
        (w_qkv, held),
        (x, rows),
        (w_out.at[:, columns(conv + y)], beta.at[0:48, :]),
        (w_glu.at[:, columns(glu + y)], beta.at[48:144, :]),
        (w_glu.at[0:48, columns(glu + 4 + y)], beta.at[144:192, :]),
        (w_conv.at[0:48, columns(conv + y)], beta.at[192:240, :]),
        (w_out.at[:, columns(conv + 4 + a)], gam.at[0:48, :]),
        (w_conv.at[:, columns(conv + 4 + a)], gam.at[432:528, :]),
    ]
    for j in range(2):
        copies.append((w_glu.at[48:96, columns(glu + 4 + 2 * a + j)], gam.at[48 + 48 * j : 96 + 48 * j, :]))
        copies.append((w_glu.at[:, columns(glu + 8 + 2 * a + j)], gam.at[144 + 96 * j : 240 + 96 * j, :]))
        copies.append((w_conv.at[48:96, columns(conv + 2 * a + j)], gam.at[336 + 48 * j : 384 + 48 * j, :]))
    wait = run_copies(copies, sems)
    beta[240:528, :] = jnp.zeros((288, LANES), BF16)
    wait()
    for j in range(HEADS):

        @pl.when(ctx == j)
        def _():
            for part in range(3):
                first = part * 768 + DH * j
                beta[240 + 96 * part : 336 + 96 * part, 0:DH] = held[:, first : first + DH]

    normed[...] = norm_rows(rows[...].astype(F32)).astype(BF16)


STEPS = (0, -1, -2, -3, 1, 2, 3)


def order_kernel(*refs):
    blocks, low, high, w, beta, gam = refs[0:7], refs[7], refs[8], refs[9], refs[10], refs[11]
    _, _, _, z, _, _ = whereabouts()

    def near(ref, at):
        for side in range(2):
            first = NEAR * side
            beta[at, 240 * side : 240 * (side + 1), :] = ref[first : first + 240, :]
            for part in range(3):
                start = first + 240 + 96 * part
                w[at, side, :, LANES * part : LANES * (part + 1)] = ref[start : start + 96, :]

    near(low, z ^ 4)
    gam[z ^ 4] = high[...]
    for ref, step in zip(blocks, STEPS):
        at = (z + step) & 7
        near(ref, at)
        gam[at] = ref[2 * NEAR :, :]


def attend_kernel(length, x, w, out, q, k, v, att):
    att[0:HALO, :] = jnp.zeros((HALO, LANES), BF16)
    att[SEQ + HALO : SEQ + 2 * HALO, :] = jnp.zeros((HALO, LANES), BF16)
    mat = w[...].reshape(D, 3 * LANES)
    for i in range(4):
        rows = slice(256 * i, 256 * (i + 1))
        made = jnp.dot(x[2 * i : 2 * i + 2].reshape(256, D), mat, preferred_element_type=F32).astype(BF16)
        for part, ref in enumerate((q, k, v)):
            ref[rows, :] = made[:, LANES * part : LANES * (part + 1)]
    valid = lax.broadcasted_iota(jnp.int32, (1, SEQ), 1) < length[0]
    keys, values = k[...], v[...]
    for i in range(HEADS):
        scores = lax.dot_general(
            q[ROWS * i : ROWS * (i + 1), :], keys, (((1,), (1,)), ((), ())), preferred_element_type=F32
        )
        scores = jnp.where(valid, scores, masked_score)
        top = jnp.max(scores, axis=-1, keepdims=True)
        exp_scores = jnp.exp((scores - top) * DH ** (-0.5))
        total = jnp.sum(exp_scores, axis=-1, keepdims=True)
        added = jnp.dot(exp_scores.astype(BF16), values, preferred_element_type=F32)
        att[HALO + ROWS * i : HALO + ROWS * (i + 1), :] = (added / total).astype(BF16)
    for i in range(HEADS):
        out[i] = att[ROWS * i : ROWS * i + WIDE, :]


def cut_kernel(beta_1, beta_3, gamma_1, gamma_3, beta_low, beta_high, gamma_low, gamma_high, sems):
    run_copies(
        [
            (beta_1.at[0:4], beta_low), (beta_3.at[4:8], beta_high),
            (gamma_1.at[0:4], gamma_low), (gamma_3.at[4:8], gamma_high),
        ],
        sems,
    )()


def halves(refs):
    whole, low, high = slice(0, 8), slice(0, 4), slice(4, 8)
    return list(zip((0, 1, 2, 2, 3), (whole, whole, low, high, whole), refs))


def middle_kernel(length, att_in, frames_in, before_in, behind_in, taps_in, *refs):
    pieces = refs[0:20]
    out, att, frames, taps, w_out, w, w_conv, ext, summed, own_sems, out_sems, glu_sems, conv_sems = refs[20:]
    own_wait = run_copies(
        [
            (att_in, att), (before_in, frames.at[0:HALO]), (frames_in, frames.at[HALO : HALO + ROWS]),
            (behind_in, frames.at[HALO + ROWS :]), (taps_in, taps),
        ],
        own_sems,
    )
    _, y, a, _, h, core = whereabouts()
    owners = [(0, core), (10, 1 - core)]

    def glu_copy(source, z, rows, h, block):
        target = w.at[z, h, rows, columns(block)]
        pltpu.make_async_copy(source, target, glu_sems.at[block]).start()

    def conv_copy(source, z, rows, h, block):
        target = w_conv.at[z, h, rows, columns(block)]
        pltpu.make_async_copy(source, target, conv_sems.at[0]).start()

    def glu_wait(block):
        target = w.at[:, :, :, LANES * block : LANES * (block + 1)]
        pltpu.make_async_copy(target, target, glu_sems.at[block]).wait()

    copies = []
    for first, at in owners:
        for i, z, ref in halves(pieces[first : first + 5]):
            for side in range(2):
                start = 240 * side
                copies.append((ref.at[:, start : start + 48, :], w_out.at[z, side, :, columns(at * 6 + (y ^ i))]))
        for i, z, ref in halves(pieces[first + 5 : first + 10]):
            copies.append((ref.at[:, 0:48, :], w_out.at[z, h ^ (i >> 1), :, columns(at * 6 + 4 + (a ^ (i & 1)))]))
    out_wait = run_copies(copies, out_sems)
    whole, low, high = slice(0, 96), slice(0, 48), slice(48, 96)
    for first, at in owners:
        for i, z, ref in halves(pieces[first : first + 5]):
            for side in range(2):
                start = 240 * side + 48
                glu_copy(ref.at[:, start : start + 96, :], z, whole, side, at * 12 + (y ^ i))
    for first, at in owners:
        for i, z, ref in halves(pieces[first : first + 5]):
            for side in range(2):
                start = 240 * side + 144
                glu_copy(ref.at[:, start : start + 48, :], z, low, side, at * 12 + 4 + (y ^ i))
        for i, z, ref in halves(pieces[first + 5 : first + 10]):
            block = at * 12 + 4 + 2 * (a ^ (i & 1))
            for j in range(2):
                start = 48 + 48 * j
                glu_copy(ref.at[:, start : start + 48, :], z, high, h ^ (i >> 1), block + j)
    for first, at in owners:
        for i, z, ref in halves(pieces[first + 5 : first + 10]):
            block = at * 12 + 8 + 2 * (a ^ (i & 1))
            for j in range(2):
                start = 144 + 96 * j
                glu_copy(ref.at[:, start : start + 96, :], z, whole, h ^ (i >> 1), block + j)

    for first, at in owners:
        for i, z, ref in halves(pieces[first : first + 5]):
            for side in range(2):
                start = 240 * side + 192
                conv_copy(ref.at[:, start : start + 48, :], z, low, side, at * 6 + (y ^ i))
        for i, z, ref in halves(pieces[first + 5 : first + 10]):
            there = a ^ (i & 1)
            for j in range(2):
                start = 336 + 48 * j
                conv_copy(ref.at[:, start : start + 48, :], z, high, h ^ (i >> 1), at * 6 + 2 * there + j)
            conv_copy(ref.at[:, 432:528, :], z, whole, h ^ (i >> 1), at * 6 + 4 + there)

    out_wait()
    own_wait()
    total = frames[...].astype(F32)
    for head in range(HEADS):
        mat = w_out[head].reshape(DH, D)
        total = total + jnp.dot(att[head][:, 0:DH], mat, preferred_element_type=F32)
    total = total.astype(BF16)
    mixed = total[HALO : HALO + ROWS]
    rows = norm_rows(total.astype(F32)).astype(BF16)

    position = lax.axis_index("ctx") * ROWS - HALO + lax.broadcasted_iota(jnp.int32, (WIDE, 1), 0)
    valid = (position >= 0) & (position < length[0])
    for n in range(6):
        for block in (2 * n, 2 * n + 1, 12 + 2 * n, 13 + 2 * n):
            glu_wait(block)
        mats = [
            w[:, :, :, at + 256 * n : at + 256 * (n + 1)].reshape(D, 256) for at in (0, D)
        ]
        value, gate = [jnp.dot(rows, mat, preferred_element_type=F32) for mat in mats]
        gated = value * jax.nn.sigmoid(gate)
        ext[:, 256 * n : 256 * (n + 1)] = jnp.where(valid, gated, 0.0).astype(BF16).astype(F32)
        for m in (2 * n, 2 * n + 1):
            cols = slice(LANES * m, LANES * (m + 1))
            total = jnp.zeros((ROWS, LANES), F32)
            tap_rows = taps[:, cols].astype(F32)
            for j in range(TAPS):
                total = total + tap_rows[j : j + 1, :] * ext[j + 1 : j + 1 + ROWS, cols]
            summed[:, cols] = total
    normed = norm_rows(summed[...])
    activated = (normed * jax.nn.sigmoid(normed)).astype(BF16)
    pltpu.make_async_copy(w_conv, w_conv, conv_sems.at[0]).wait()
    for n in range(6):
        cols = slice(256 * n, 256 * (n + 1))
        mat = w_conv[:, :, :, cols].reshape(D, 256)
        total = mixed[:, cols].astype(F32) + jnp.dot(activated, mat, preferred_element_type=F32)
        out[:, cols] = total.astype(BF16)


def shape(*dims, dtype=BF16):
    return jax.ShapeDtypeStruct(dims, dtype)


def ring_z(own, low, high):
    below, above = [own], [own]
    for _ in range(3):
        below.append(send(below[-1], shift_z(1)))
        above.append(send(above[-1], shift_z(-1)))
    return below + above[1:] + [send(low(below[3]), shift_z(1)), send(high(above[3]), shift_z(-1))]


def per_device(frames, lengths, w_qkv, w_out, w_glu, depth_kernel, w_conv_out):
    frame_rows = frames[0]
    near, gamma, normed = pl.pallas_call(
        pack_kernel,
        out_shape=(shape(NEAR, LANES), shape(GAMMA, LANES), shape(ROWS, D)),
        in_specs=[ANY] * 5,
        out_specs=(VM,) * 3,
        scratch_shapes=[
            pltpu.VMEM((96, 2304), BF16), pltpu.VMEM((ROWS, D), BF16), pltpu.SemaphoreType.DMA((14,))
        ],
        compiler_params=params(),
    )(frame_rows, w_qkv, w_out, w_glu, w_conv_out)
    far = send(near, SWAP_H)
    every = lax.all_to_all(jnp.broadcast_to(normed[None], (8, ROWS, D)), "ctx", 0, 0)

    _, _, _, _, h, _ = whereabouts()
    pack = jnp.concatenate([jnp.where(h == 0, near, far), jnp.where(h == 0, far, near), gamma], axis=0)
    blocks = ring_z(pack, lambda v: v[: 2 * NEAR], lambda v: v[2 * NEAR :])
    w_head, beta, gamma = pl.pallas_call(
        order_kernel,
        out_shape=(shape(8, 2, 96, 3 * LANES), shape(8, BETA, LANES), shape(8, GAMMA, LANES)),
        in_specs=[VM] * 9,
        out_specs=(VM,) * 3,
        compiler_params=params(16),
    )(*blocks)

    gamma_1, gamma_3 = send(gamma, xor_x(1)), send(gamma, xor_x(3))
    beta_1, beta_3 = send(beta, xor_y(1)), send(beta, xor_y(3))
    beta_other, gamma_other = send(beta, SWAP_CORE), send(gamma, SWAP_CORE)

    att = pl.pallas_call(
        attend_kernel,
        out_shape=shape(8, WIDE, LANES),
        in_specs=[SM, VM, VM],
        out_specs=VM,
        scratch_shapes=[
            pltpu.VMEM((SEQ, LANES), BF16),
            pltpu.VMEM((SEQ, LANES), BF16),
            pltpu.VMEM((SEQ, LANES), BF16),
            pltpu.VMEM((SEQ + 2 * HALO, LANES), BF16),
        ],
        cost_estimate=cost(2 * 10**10),
        compiler_params=params(16),
    )(lengths, every, after(w_head, beta_other, gamma_other))

    up = [(i, i + 1) for i in range(7)]
    down = [(i + 1, i) for i in range(7)]
    halo = after(frame_rows, att)
    att = lax.all_to_all(att, "ctx", 0, 0)
    frames_before = lax.ppermute(halo[ROWS - HALO :], "ctx", up)
    frames_behind = lax.ppermute(halo[:HALO], "ctx", down)
    beta_1, beta_3, gamma_1, gamma_3, att, frames_before, frames_behind = lax.optimization_barrier(
        (beta_1, beta_3, gamma_1, gamma_3, att, frames_before, frames_behind)
    )
    beta_2, beta_2b, gamma_2, gamma_2b = pl.pallas_call(
        cut_kernel,
        out_shape=(shape(4, BETA, LANES),) * 2 + (shape(4, GAMMA, LANES),) * 2,
        in_specs=[ANY] * 4,
        out_specs=(VM,) * 4,
        scratch_shapes=[pltpu.SemaphoreType.DMA((4,))],
        compiler_params=params(16),
    )(beta_1, beta_3, gamma_1, gamma_3)
    beta_2, beta_2b = send(beta_2, xor_y(3)), send(beta_2b, xor_y(1))
    gamma_2, gamma_2b = send(gamma_2, xor_x(3)), send(gamma_2b, xor_x(1))
    swapped_1 = [send(v, SWAP_CORE) for v in (beta_1, beta_3, gamma_1, gamma_3)]
    second = [beta_2, beta_2b, gamma_2, gamma_2b]
    swapped_2 = [send(v, SWAP_CORE) for v in second]
    pieces = [
        beta, beta_1, beta_2, beta_2b, beta_3, gamma, gamma_1, gamma_2, gamma_2b, gamma_3,
        beta_other, swapped_1[0], swapped_2[0], swapped_2[1], swapped_1[1],
        gamma_other, swapped_1[2], swapped_2[2], swapped_2[3], swapped_1[3],
    ]

    result = pl.pallas_call(
        middle_kernel,
        out_shape=shape(ROWS, D),
        in_specs=[SM] + [ANY] * 25,
        out_specs=VM,
        scratch_shapes=[
            pltpu.VMEM((8, WIDE, LANES), BF16),
            pltpu.VMEM((WIDE, D), BF16),
            pltpu.VMEM((TAPS, D), BF16),
            pltpu.VMEM((8, 2, 48, D), BF16),
            pltpu.VMEM((8, 2, 96, 2 * D), BF16),
            pltpu.VMEM((8, 2, 96, D), BF16),
            pltpu.VMEM((WIDE, D), F32),
            pltpu.VMEM((ROWS, D), F32),
            pltpu.SemaphoreType.DMA((5,)),
            pltpu.SemaphoreType.DMA((30,)),
            pltpu.SemaphoreType.DMA((24,)),
            pltpu.SemaphoreType.DMA((1,)),
        ],
        compiler_params=params(26),
    )(lengths, att, frame_rows, frames_before, frames_behind, depth_kernel, *pieces)
    return result[None]


def solution(mesh):
    in_specs = (
        P(("dp", "fsdp"), "ctx", None),
        P(("dp", "fsdp")),
        P("fsdp", None),
        P("fsdp", None),
        P("fsdp", None),
        P(),
        P("fsdp", None),
    )
    out_specs = P(("dp", "fsdp"), "ctx", None)
    return jax.shard_map(
        per_device, mesh=mesh, in_specs=in_specs, out_specs=out_specs, check_vma=False
    )
```

time: 580 us -> 137 us (0.24)
  waiting for transfers between devices: 520 us -> 51.2 us
  starting transfers between devices: 7.59 us -> 49.2 us
  Pallas kernels: 0 us -> 25.8 us
  matrix products: 21.9 us -> 0 us
  between operations: 14.3 us -> 1.05 us
  other arithmetic: 7.55 us -> 0.06 us
    all_gather x6 -> x0, waiting for transfers between devices: 517 us -> none  [the longest x1 146 us: glu_product(): return fold_into(operand, lax.all_gather(w_glu, 'fsdp', axis=0, tiled=True))]
    ppermute x2 -> x29, waiting for transfers between devices: 0.95 us -> 51.2 us  [the longest x27 45.2 us: send(): return lax.ppermute(value, AXES, moves)]
    ppermute x2 -> x29, starting transfers between devices: 7.39 us -> 38.7 us  [the longest x27 32.5 us: send(): return lax.ppermute(value, AXES, moves)]
    pallas_call x0 -> x5, Pallas kernels: none -> 25.8 us  [the longest x1 13.9 us: per_device(): pl.pallas_call(middle_kernel, out_shape=shape(ROWS, D), in_specs=[SM] + [...]
    dot_general x6 -> x0, matrix products: 21.9 us -> none  [the longest x4 15.7 us: fold_into(): return jnp.dot(operand, shard_piece, preferred_element_type=jnp.float32)]
    all_to_all x0 -> x2, starting transfers between devices: none -> 10.5 us  [the longest x1 5.64 us: per_device(): lax.all_to_all(jnp.broadcast_to(normed[None], (8, ROWS, D)), 'ctx', 0, 0)]
    reduce_sum x6 -> x0, other arithmetic: 7.12 us -> none  [the longest x2 4.37 us: layer_norm(): middle = jnp.mean(values, axis=-1, keepdims=True)]
  transfers between devices with their start and end apart: 8 -> 31, of which waited for: 7 -> 15; matrix products, arithmetic and copies ran while one was open for 4% -> 2% of each run, Pallas kernels for 0% -> 6%
where the time goes in v1:
time: 137 us
  waiting for transfers between devices  51.2 us (37%)
  starting transfers between devices  49.2 us (36%)
  Pallas kernels  25.8 us (19%)
  local copies, waits for them, and re-layouts  9.29 us (7%)
    ppermute x27, waiting for transfers between devices, send(): return lax.ppermute(value, AXES, moves)  45.2 us
    ppermute x27, starting transfers between devices, send(): return lax.ppermute(value, AXES, moves)  32.5 us
    pallas_call x1, Pallas kernels, per_device(): pl.pallas_call(middle_kernel, out_shape=shape(ROWS, D), in_specs=[SM] + [...  13.9 us
    pallas_call x1, Pallas kernels, per_device(): pl.pallas_call(attend_kernel, out_shape=shape(8, WIDE, LANES), in_specs=[...  6.62 us
    unnamed x30, local copies, waits for them, and re-layouts  6.32 us
    all_to_all x1, starting transfers between devices, per_device(): lax.all_to_all(jnp.broadcast_to(normed[None], (8, ROWS, D)), 'ctx', 0, 0)  5.64 us
    all_to_all x1, starting transfers between devices, per_device(): att = lax.all_to_all(att, 'ctx', 0, 0)  4.83 us
    ppermute x1, starting transfers between devices, per_device(): frames_behind = lax.ppermute(halo[:HALO], 'ctx', down)  4.3 us
  transfers between devices with their start and end apart: 31, of which 15 were waited for; matrix products, arithmetic and copies ran while one was open for 2% of the time, Pallas kernels for 6%

profile of v1, /device:TPU:3, one launch (start us, length us, event | category | flops | bytes accessed | tf_op | source)
XLA Modules:
  0.0 136.6 jit_solution(10619502768808784034)
XLA Ops:
  0.0 2.3 %shard_map.73 = (bf16[528,128]{1,0:T(8,128)(2,1)}, bf16[528,128]{1,0:T(8,128)(2,1)}, bf16[128,1536]{1,0:T(8,128)(2,1)}) custom-call(bf16[128,1536]{1,0:T(8,128)(2,1)} %bitcast.2, bf16[96,2304]{1,0:T(8,128)(2,1)} %w_qkv.1, bf16[48,1536]{1,0:T(8,128)(2,1)} %w_out.1, bf16[96,3072]{1,0:T(8,128)(2,1)} %w_glu.1, bf16[96,1536]{1,0:T(8,128)(2,1)} %w_conv.1), custom_call_target="tpu_custom_call" | custom-call | tf_op jit(solution)/shard_map/pallas_call | solution.py:317
  2.3 1.9 %collective-permute-start = (bf16[528,128]{1,0:T(8,128)(2,1)}, bf16[528,128]{1,0:T(8,128)(2,1)S(1)}, u32[]{:S(2)}, u32[]{:S(2)}) collective-permute-start(bf16[528,128]{1,0:T(8,128)(2,1)} %get-tuple-element.24), channel_id=1, source_target_pairs={{0,2},{1,3},{2,0},{3,1},{4,6},{5,7},{6,4},{7,5},{8,10},{9,11},{10,... | collective-permute-start | bytes 405512 | tf_op jit(solution)/shard_map/ppermute | solution.py:50
  4.3 2.9 %broadcast_in_dim.4 = bf16[8,128,1536]{2,1,0:T(8,128)(2,1)} broadcast(bf16[128,1536]{1,0:T(8,128)(2,1)} %get-tuple-element.28), dimensions={1,2} | broadcast | bytes 3538944 | tf_op jit(solution)/shard_map/broadcast_in_dim | solution.py:328
  7.2 5.6 %all-to-all-start = ((bf16[8,128,1536]{2,1,0:T(8,128)(2,1)}), bf16[8,128,1536]{2,1,0:T(8,128)(2,1)}, u32[]{:S(2)}, u32[]{:S(2)}) async-start(bf16[8,128,1536]{2,1,0:T(8,128)(2,1)} %broadcast_in_dim.4), calls=%async_computation | async-start | bytes 6291456 | tf_op jit(solution)/shard_map/all_to_all | solution.py:328
  12.9 1.7 %collective-permute-start.1 = (bf16[1584,128]{1,0:T(8,128)(2,1)S(1)}, bf16[1584,128]{1,0:T(8,128)(2,1)S(1)}, u32[]{:S(2)}, u32[]{:S(2)}) collective-permute-start(bf16[1584,128]{1,0:T(8,128)(2,1)S(1)} %pad_maximum_fusion.refs_0_), channel_id=1, source_target_pairs={{0,4},{1,5},{2,6},{3,7},{4,8},{5,9},{6,10},{7,11},{8,12},{9,13},{1... | collective-permute-start | bytes 1216520 | tf_op jit(solution)/shard_map/ppermute | solution.py:50
  14.7 4.0 %collective-permute-start.4 = (bf16[1584,128]{1,0:T(8,128)(2,1)S(1)}, bf16[1584,128]{1,0:T(8,128)(2,1)S(1)}, u32[]{:S(2)}, u32[]{:S(2)}) collective-permute-start(bf16[1584,128]{1,0:T(8,128)(2,1)S(1)} %pad_maximum_fusion.refs_0_), channel_id=1, source_target_pairs={{0,28},{1,29},{2,30},{3,31},{4,0},{5,1},{6,2},{7,3},{8,4},{9,5},{1... | collective-permute-start | bytes 1216520 | tf_op jit(solution)/shard_map/ppermute | solution.py:50
  18.7 8.2 %collective-permute-done.1.refs_1_ = bf16[1584,128]{1,0:T(8,128)(2,1)S(1)} collective-permute-done((bf16[1584,128]{1,0:T(8,128)(2,1)S(1)}, bf16[1584,128]{1,0:T(8,128)(2,1)S(1)}, u32[]{:S(2)}, u32[]{:S(2)}) %collective-permute-start.1) | collective-permute-done | bytes 405536 | tf_op jit(solution)/shard_map/ppermute | solution.py:50
  26.9 2.7 %collective-permute-start.5 = (bf16[1584,128]{1,0:T(8,128)(2,1)S(1)}, bf16[1584,128]{1,0:T(8,128)(2,1)S(1)}, u32[]{:S(2)}, u32[]{:S(2)}) collective-permute-start(bf16[1584,128]{1,0:T(8,128)(2,1)S(1)} %collective-permute-done.4.refs_4_), channel_id=1, source_target_pairs={{0,28},{1,29},{2,30},{3,31},{4,0},{5,1},{6,2},{7,3},{8,4},{9,5},{1... | collective-permute-start | bytes 1216520 | tf_op jit(solution)/shard_map/ppermute | solution.py:50
  29.6 7.5 %collective-permute-done.2.refs_2_ = bf16[1584,128]{1,0:T(8,128)(2,1)S(1)} collective-permute-done((bf16[1584,128]{1,0:T(8,128)(2,1)S(1)}, bf16[1584,128]{1,0:T(8,128)(2,1)S(1)}, u32[]{:S(2)}, u32[]{:S(2)}) %collective-permute-start.2) | collective-permute-done | bytes 405536 | tf_op jit(solution)/shard_map/ppermute | solution.py:50
  37.1 2.7 %collective-permute-start.6 = (bf16[1584,128]{1,0:T(8,128)(2,1)S(1)}, bf16[1584,128]{1,0:T(8,128)(2,1)S(1)}, u32[]{:S(2)}, u32[]{:S(2)}) collective-permute-start(bf16[1584,128]{1,0:T(8,128)(2,1)S(1)} %collective-permute-done.5.refs_5_), channel_id=1, source_target_pairs={{0,28},{1,29},{2,30},{3,31},{4,0},{5,1},{6,2},{7,3},{8,4},{9,5},{1... | collective-permute-start | bytes 1216520 | tf_op jit(solution)/shard_map/ppermute | solution.py:50
  39.8 6.7 %collective-permute-done.3.refs_3_ = bf16[1584,128]{1,0:T(8,128)(2,1)S(1)} collective-permute-done((bf16[1584,128]{1,0:T(8,128)(2,1)S(1)}, bf16[1584,128]{1,0:T(8,128)(2,1)S(1)}, u32[]{:S(2)}, u32[]{:S(2)}) %collective-permute-start.3) | collective-permute-done | bytes 405536 | tf_op jit(solution)/shard_map/ppermute | solution.py:50
  46.6 2.7 %collective-permute-start.8 = (bf16[528,128]{1,0:T(8,128)(2,1)S(1)}, bf16[528,128]{1,0:T(8,128)(2,1)S(1)}, u32[]{:S(2)}, u32[]{:S(2)}) collective-permute-start(bf16[528,128]{1,0:T(8,128)(2,1)S(1)} %slice.17), channel_id=1, source_target_pairs={{0,28},{1,29},{2,30},{3,31},{4,0},{5,1},{6,2},{7,3},{8,4},{9,5},{1... | collective-permute-start | bytes 405512 | tf_op jit(solution)/shard_map/ppermute | solution.py:50
  49.4 2.0 %collective-permute-done.8.refs_8_ = bf16[528,128]{1,0:T(8,128)(2,1)S(1)} collective-permute-done((bf16[528,128]{1,0:T(8,128)(2,1)S(1)}, bf16[528,128]{1,0:T(8,128)(2,1)S(1)}, u32[]{:S(2)}, u32[]{:S(2)}) %collective-permute-start.8) | collective-permute-done | bytes 135200 | tf_op jit(solution)/shard_map/ppermute | solution.py:50
  51.4 1.8 %collective-permute-done.7.refs_7_ = bf16[1056,128]{1,0:T(8,128)(2,1)S(1)} collective-permute-done((bf16[1056,128]{1,0:T(8,128)(2,1)S(1)}, bf16[1056,128]{1,0:T(8,128)(2,1)S(1)}, u32[]{:S(2)}, u32[]{:S(2)}) %collective-permute-start.7) | collective-permute-done | bytes 270368 | tf_op jit(solution)/shard_map/ppermute | solution.py:50
  53.1 1.8 %shard_map.74 = (bf16[8,2,96,384]{3,2,1,0:T(8,128)(2,1)S(1)}, bf16[8,480,128]{2,1,0:T(8,128)(2,1)}, bf16[8,528,128]{2,1,0:T(8,128)(2,1)}) custom-call(bf16[1584,128]{1,0:T(8,128)(2,1)S(1)} %pad_maximum_fusion.refs_0_, bf16[1584,128]{1,0:T(8,128)(2,1)S(1)} %collective-permute-done.1.refs_1_, bf16[1584,128]{1,0:T(8,128)(2,1)S(1)} %collective-permute-done.2.refs_2_, ...), custom_call_target="tpu_custom_call" | custom-call | tf_op jit(solution)/shard_map/pallas_call | solution.py:333
  54.9 1.0 copy-done.11
  55.9 4.8 %collective-permute-start.14 = (bf16[8,528,128]{2,1,0:T(8,128)(2,1)}, bf16[8,528,128]{2,1,0:T(8,128)(2,1)S(1)}, u32[]{:S(2)}, u32[]{:S(2)}) collective-permute-start(bf16[8,528,128]{2,1,0:T(8,128)(2,1)} %get-tuple-element.27.refs_5_), channel_id=1, source_target_pairs={{0,1},{1,0},{2,3},{3,2},{4,5},{5,4},{6,7},{7,6},{8,9},{9,8},{10,11... | collective-permute-start | bytes 3244040 | tf_op jit(solution)/shard_map/ppermute | solution.py:50
  61.4 2.5 %collective-permute-start.10 = (bf16[8,480,128]{2,1,0:T(8,128)(2,1)}, bf16[8,480,128]{2,1,0:T(8,128)(2,1)S(1)}, u32[]{:S(2)}, u32[]{:S(2)}) collective-permute-start(bf16[8,480,128]{2,1,0:T(8,128)(2,1)} %get-tuple-element.26.refs_0_), channel_id=1, source_target_pairs={{0,96},{1,97},{2,98},{3,99},{4,100},{5,101},{6,102},{7,103},{8,104... | collective-permute-start | bytes 2949128 | tf_op jit(solution)/shard_map/ppermute | solution.py:50
  63.9 0.8 collective-permute-done.13.refs_10_
  64.7 1.0 copy-done.3
  65.7 1.0 collective-permute-start.11
  66.7 1.0 copy-done.1
  67.7 1.3 copy-done.12
  69.0 6.6 %shard_map.75 = bf16[8,160,128]{2,1,0:T(8,128)(2,1)S(1)} custom-call(s32[1]{0:T(128)S(6)} %copy.8.length, bf16[8,128,1536]{2,1,0:T(8,128)(2,1)} %all-to-all-done.x, bf16[8,2,96,384]{3,2,1,0:T(8,128)(2,1)S(1)} %copy-done.12), custom_call_target="tpu_custom_call" | custom-call | flops 20000000000 | bytes 1048576 | tf_op jit(solution)/shard_map/pallas_call | solution.py:345
  75.6 0.7 copy-done.5
  76.4 4.8 %all-to-all-start.1 = ((bf16[8,160,128]{2,1,0:T(8,128)(2,1)}), bf16[8,160,128]{2,1,0:T(8,128)(2,1)}, u32[]{:S(2)}, u32[]{:S(2)}) async-start(bf16[8,160,128]{2,1,0:T(8,128)(2,1)} %copy-done.5), calls=%async_computation.1 | async-start | bytes 655360 | tf_op jit(solution)/shard_map/all_to_all | solution.py:363
  81.2 4.3 %collective-permute-start.16 = (bf16[16,1536]{1,0:T(8,128)(2,1)S(1)}, bf16[16,1536]{1,0:T(8,128)(2,1)S(1)}, u32[]{:S(2)}, u32[]{:S(2)}) collective-permute-start(bf16[16,1536]{1,0:T(8,128)(2,1)S(1)} %get-tuple-element.43), channel_id=1, source_target_pairs={{32,0},{64,32},{96,64},{128,96},{160,128},{192,160},{224,192},{33,... | collective-permute-start | bytes 147464 | tf_op jit(solution)/shard_map/ppermute | solution.py:365
  85.7 1.9 %collective-permute-start.15 = (bf16[16,1536]{1,0:T(8,128)(2,1)S(1)}, bf16[16,1536]{1,0:T(8,128)(2,1)S(1)}, u32[]{:S(2)}, u32[]{:S(2)}) collective-permute-start(bf16[16,1536]{1,0:T(8,128)(2,1)S(1)} %get-tuple-element.44), channel_id=1, source_target_pairs={{0,32},{32,64},{64,96},{96,128},{128,160},{160,192},{192,224},{1,3... | collective-permute-start | bytes 147464 | tf_op jit(solution)/shard_map/ppermute | solution.py:364
  87.6 1.1 collective-permute-done.12.gamma_3.refs_9_
  88.7 2.1 %collective-permute-done.11.gamma_1.refs_6_ = bf16[8,528,128]{2,1,0:T(8,128)(2,1)S(1)} collective-permute-done((bf16[8,528,128]{2,1,0:T(8,128)(2,1)}, bf16[8,528,128]{2,1,0:T(8,128)(2,1)S(1)}, u32[]{:S(2)}, u32[]{:S(2)}) %collective-permute-start.11) | collective-permute-done | bytes 1081376 | tf_op jit(solution)/shard_map/ppermute | solution.py:50
  90.8 2.6 %collective-permute-done.16.behind_in = bf16[16,1536]{1,0:T(8,128)(2,1)S(1)} collective-permute-done((bf16[16,1536]{1,0:T(8,128)(2,1)S(1)}, bf16[16,1536]{1,0:T(8,128)(2,1)S(1)}, u32[]{:S(2)}, u32[]{:S(2)}) %collective-permute-start.16) | collective-permute-done | bytes 49184 | tf_op jit(solution)/shard_map/ppermute | solution.py:365
  93.4 0.6 copy-done.7
  94.0 3.4 %collective-permute-done.15.before_in = bf16[16,1536]{1,0:T(8,128)(2,1)S(1)} collective-permute-done((bf16[16,1536]{1,0:T(8,128)(2,1)S(1)}, bf16[16,1536]{1,0:T(8,128)(2,1)S(1)}, u32[]{:S(2)}, u32[]{:S(2)}) %collective-permute-start.15) | collective-permute-done | bytes 49184 | tf_op jit(solution)/shard_map/ppermute | solution.py:364
  97.5 0.6 copy-done.9
  98.1 1.2 shard_map.76
  99.4 0.8 collective-permute-start.19
  100.2 1.1 collective-permute-start.20
  101.3 2.2 %collective-permute-start.21 = (bf16[8,480,128]{2,1,0:T(8,128)(2,1)}, bf16[8,480,128]{2,1,0:T(8,128)(2,1)S(1)}, u32[]{:S(2)}, u32[]{:S(2)}) collective-permute-start(bf16[8,480,128]{2,1,0:T(8,128)(2,1)} %collective-permute-done.9.beta_1.refs_1_), channel_id=1, source_target_pairs={{0,1},{1,0},{2,3},{3,2},{4,5},{5,4},{6,7},{7,6},{8,9},{9,8},{10,11... | collective-permute-start | bytes 2949128 | tf_op jit(solution)/shard_map/ppermute | solution.py:50
  103.5 8.4 %collective-permute-done.17.refs_2_ = bf16[4,480,128]{2,1,0:T(8,128)(2,1)S(1)} collective-permute-done((bf16[4,480,128]{2,1,0:T(8,128)(2,1)S(1)}, bf16[4,480,128]{2,1,0:T(8,128)(2,1)S(1)}, u32[]{:S(2)}, u32[]{:S(2)}) %collective-permute-start.17) | collective-permute-done | bytes 491552 | tf_op jit(solution)/shard_map/ppermute | solution.py:50
  111.9 2.3 %collective-permute-start.24 = (bf16[8,480,128]{2,1,0:T(8,128)(2,1)S(1)}, bf16[8,480,128]{2,1,0:T(8,128)(2,1)S(1)}, u32[]{:S(2)}, u32[]{:S(2)}) collective-permute-start(bf16[8,480,128]{2,1,0:T(8,128)(2,1)S(1)} %collective-permute-done.10.beta_3.refs_4_), channel_id=1, source_target_pairs={{0,1},{1,0},{2,3},{3,2},{4,5},{5,4},{6,7},{7,6},{8,9},{9,8},{10,11... | collective-permute-start | bytes 2949128 | tf_op jit(solution)/shard_map/ppermute | solution.py:50
  114.3 0.5 collective-permute-start.28
  114.9 0.4 collective-permute-start.26
  115.3 1.2 collective-permute-done.24.refs_14_
  116.5 0.4 collective-permute-start.27
  116.8 3.4 %collective-permute-done.22.refs_12_ = bf16[4,480,128]{2,1,0:T(8,128)(2,1)S(1)} collective-permute-done((bf16[4,480,128]{2,1,0:T(8,128)(2,1)S(1)}, bf16[4,480,128]{2,1,0:T(8,128)(2,1)S(1)}, u32[]{:S(2)}, u32[]{:S(2)}) %collective-permute-start.22) | collective-permute-done | bytes 491552 | tf_op jit(solution)/shard_map/ppermute | solution.py:50
  120.3 0.4 collective-permute-start.23
  120.6 1.9 %collective-permute-done.23.refs_13_ = bf16[4,480,128]{2,1,0:T(8,128)(2,1)S(1)} collective-permute-done((bf16[4,480,128]{2,1,0:T(8,128)(2,1)S(1)}, bf16[4,480,128]{2,1,0:T(8,128)(2,1)S(1)}, u32[]{:S(2)}, u32[]{:S(2)}) %collective-permute-start.23) | collective-permute-done | bytes 491552 | tf_op jit(solution)/shard_map/ppermute | solution.py:50
  122.6 13.9 %shard_map.77 = bf16[128,1536]{1,0:T(8,128)(2,1)} custom-call(s32[1]{0:T(128)S(6)} %copy.8.length, bf16[8,160,128]{2,1,0:T(8,128)(2,1)} %all-to-all-done.1.att_in, bf16[128,1536]{1,0:T(8,128)(2,1)S(1)} %bitcast.4, bf16[16,1536]{1,0:T(8,128)(2,1)S(1)} %copy-done.10, bf16[16,1536]{1,0:T(8,128)(2,1)S(1)} %copy-done.8, bf16[31,1536]{1,0:T(8,128)(2,1)S(1)} %copy-done.6, ...), custom_call_target="tpu_custom_call" | custom-call | tf_op jit(solution)/shard_map/pallas_call | solution.py:388
  (55 shorter events, 0.7 us)
Async XLA Ops:
  2.3 10.5 %collective-permute-start = (bf16[528,128]{1,0:T(8,128)(2,1)}, bf16[528,128]{1,0:T(8,128)(2,1)S(1)}, u32[]{:S(2)}, u32[]{:S(2)}) collective-permute-start(bf16[528,128]{1,0:T(8,128)(2,1)} %get-tuple-element.24), channel_id=1, source_target_pairs={{0,2},{1,3},{2,0},{3,1},{4,6},{5,7},{6,4},{7,5},{8,10},{9,11},{10,... | collective-permute-start | bytes 405512 | tf_op jit(solution)/shard_map/ppermute | solution.py:50
  7.2 5.7 %copy-start.14 = (bf16[528,128]{1,0:T(8,128)(2,1)S(1)}, bf16[528,128]{1,0:T(8,128)(2,1)}, u32[]{:S(2)}) copy-start(bf16[528,128]{1,0:T(8,128)(2,1)} %get-tuple-element.24) | copy-start | bytes 405508
  7.2 5.7 %copy-start.13 = (bf16[528,128]{1,0:T(8,128)(2,1)S(1)}, bf16[528,128]{1,0:T(8,128)(2,1)}, u32[]{:S(2)}) copy-start(bf16[528,128]{1,0:T(8,128)(2,1)} %get-tuple-element.25) | copy-start | bytes 405508
  7.2 60.5 %all-to-all-start = ((bf16[8,128,1536]{2,1,0:T(8,128)(2,1)}), bf16[8,128,1536]{2,1,0:T(8,128)(2,1)}, u32[]{:S(2)}, u32[]{:S(2)}) async-start(bf16[8,128,1536]{2,1,0:T(8,128)(2,1)} %broadcast_in_dim.4), calls=%async_computation | async-start | bytes 6291456 | tf_op jit(solution)/shard_map/all_to_all | solution.py:328
  12.9 14.0 %collective-permute-start.1 = (bf16[1584,128]{1,0:T(8,128)(2,1)S(1)}, bf16[1584,128]{1,0:T(8,128)(2,1)S(1)}, u32[]{:S(2)}, u32[]{:S(2)}) collective-permute-start(bf16[1584,128]{1,0:T(8,128)(2,1)S(1)} %pad_maximum_fusion.refs_0_), channel_id=1, source_target_pairs={{0,4},{1,5},{2,6},{3,7},{4,8},{5,9},{6,10},{7,11},{8,12},{9,13},{1... | collective-permute-start | bytes 1216520 | tf_op jit(solution)/shard_map/ppermute | solution.py:50
  14.7 12.3 %collective-permute-start.4 = (bf16[1584,128]{1,0:T(8,128)(2,1)S(1)}, bf16[1584,128]{1,0:T(8,128)(2,1)S(1)}, u32[]{:S(2)}, u32[]{:S(2)}) collective-permute-start(bf16[1584,128]{1,0:T(8,128)(2,1)S(1)} %pad_maximum_fusion.refs_0_), channel_id=1, source_target_pairs={{0,28},{1,29},{2,30},{3,31},{4,0},{5,1},{6,2},{7,3},{8,4},{9,5},{1... | collective-permute-start | bytes 1216520 | tf_op jit(solution)/shard_map/ppermute | solution.py:50
  26.9 10.2 %collective-permute-start.2 = (bf16[1584,128]{1,0:T(8,128)(2,1)S(1)}, bf16[1584,128]{1,0:T(8,128)(2,1)S(1)}, u32[]{:S(2)}, u32[]{:S(2)}) collective-permute-start(bf16[1584,128]{1,0:T(8,128)(2,1)S(1)} %collective-permute-done.1.refs_1_), channel_id=1, source_target_pairs={{0,4},{1,5},{2,6},{3,7},{4,8},{5,9},{6,10},{7,11},{8,12},{9,13},{1... | collective-permute-start | bytes 1216520 | tf_op jit(solution)/shard_map/ppermute | solution.py:50
  26.9 10.2 %collective-permute-start.5 = (bf16[1584,128]{1,0:T(8,128)(2,1)S(1)}, bf16[1584,128]{1,0:T(8,128)(2,1)S(1)}, u32[]{:S(2)}, u32[]{:S(2)}) collective-permute-start(bf16[1584,128]{1,0:T(8,128)(2,1)S(1)} %collective-permute-done.4.refs_4_), channel_id=1, source_target_pairs={{0,28},{1,29},{2,30},{3,31},{4,0},{5,1},{6,2},{7,3},{8,4},{9,5},{1... | collective-permute-start | bytes 1216520 | tf_op jit(solution)/shard_map/ppermute | solution.py:50
  37.1 9.4 %collective-permute-start.3 = (bf16[1584,128]{1,0:T(8,128)(2,1)S(1)}, bf16[1584,128]{1,0:T(8,128)(2,1)S(1)}, u32[]{:S(2)}, u32[]{:S(2)}) collective-permute-start(bf16[1584,128]{1,0:T(8,128)(2,1)S(1)} %collective-permute-done.2.refs_2_), channel_id=1, source_target_pairs={{0,4},{1,5},{2,6},{3,7},{4,8},{5,9},{6,10},{7,11},{8,12},{9,13},{1... | collective-permute-start | bytes 1216520 | tf_op jit(solution)/shard_map/ppermute | solution.py:50
  37.1 9.5 %collective-permute-start.6 = (bf16[1584,128]{1,0:T(8,128)(2,1)S(1)}, bf16[1584,128]{1,0:T(8,128)(2,1)S(1)}, u32[]{:S(2)}, u32[]{:S(2)}) collective-permute-start(bf16[1584,128]{1,0:T(8,128)(2,1)S(1)} %collective-permute-done.5.refs_5_), channel_id=1, source_target_pairs={{0,28},{1,29},{2,30},{3,31},{4,0},{5,1},{6,2},{7,3},{8,4},{9,5},{1... | collective-permute-start | bytes 1216520 | tf_op jit(solution)/shard_map/ppermute | solution.py:50
  46.5 6.6 %collective-permute-start.7 = (bf16[1056,128]{1,0:T(8,128)(2,1)S(1)}, bf16[1056,128]{1,0:T(8,128)(2,1)S(1)}, u32[]{:S(2)}, u32[]{:S(2)}) collective-permute-start(bf16[1056,128]{1,0:T(8,128)(2,1)S(1)} %slice.16), channel_id=1, source_target_pairs={{0,4},{1,5},{2,6},{3,7},{4,8},{5,9},{6,10},{7,11},{8,12},{9,13},{1... | collective-permute-start | bytes 811016 | tf_op jit(solution)/shard_map/ppermute | solution.py:50
  46.6 4.7 %collective-permute-start.8 = (bf16[528,128]{1,0:T(8,128)(2,1)S(1)}, bf16[528,128]{1,0:T(8,128)(2,1)S(1)}, u32[]{:S(2)}, u32[]{:S(2)}) collective-permute-start(bf16[528,128]{1,0:T(8,128)(2,1)S(1)} %slice.17), channel_id=1, source_target_pairs={{0,28},{1,29},{2,30},{3,31},{4,0},{5,1},{6,2},{7,3},{8,4},{9,5},{1... | collective-permute-start | bytes 405512 | tf_op jit(solution)/shard_map/ppermute | solution.py:50
  54.9 1.0 copy-start.11
  55.9 10.8 %collective-permute-start.14 = (bf16[8,528,128]{2,1,0:T(8,128)(2,1)}, bf16[8,528,128]{2,1,0:T(8,128)(2,1)S(1)}, u32[]{:S(2)}, u32[]{:S(2)}) collective-permute-start(bf16[8,528,128]{2,1,0:T(8,128)(2,1)} %get-tuple-element.27.refs_5_), channel_id=1, source_target_pairs={{0,1},{1,0},{2,3},{3,2},{4,5},{5,4},{6,7},{7,6},{8,9},{9,8},{10,11... | collective-permute-start | bytes 3244040 | tf_op jit(solution)/shard_map/ppermute | solution.py:50
  60.7 4.0 %collective-permute-start.13 = (bf16[8,480,128]{2,1,0:T(8,128)(2,1)}, bf16[8,480,128]{2,1,0:T(8,128)(2,1)S(1)}, u32[]{:S(2)}, u32[]{:S(2)}) collective-permute-start(bf16[8,480,128]{2,1,0:T(8,128)(2,1)} %get-tuple-element.26.refs_0_), channel_id=1, source_target_pairs={{0,1},{1,0},{2,3},{3,2},{4,5},{5,4},{6,7},{7,6},{8,9},{9,8},{10,11... | collective-permute-start | bytes 2949128 | tf_op jit(solution)/shard_map/ppermute | solution.py:50
  61.4 24.3 %collective-permute-start.10 = (bf16[8,480,128]{2,1,0:T(8,128)(2,1)}, bf16[8,480,128]{2,1,0:T(8,128)(2,1)S(1)}, u32[]{:S(2)}, u32[]{:S(2)}) collective-permute-start(bf16[8,480,128]{2,1,0:T(8,128)(2,1)} %get-tuple-element.26.refs_0_), channel_id=1, source_target_pairs={{0,96},{1,97},{2,98},{3,99},{4,100},{5,101},{6,102},{7,103},{8,104... | collective-permute-start | bytes 2949128 | tf_op jit(solution)/shard_map/ppermute | solution.py:50
  63.9 23.7 %collective-permute-start.9 = (bf16[8,480,128]{2,1,0:T(8,128)(2,1)}, bf16[8,480,128]{2,1,0:T(8,128)(2,1)}, u32[]{:S(2)}, u32[]{:S(2)}) collective-permute-start(bf16[8,480,128]{2,1,0:T(8,128)(2,1)} %get-tuple-element.26.refs_0_), channel_id=1, source_target_pairs={{0,32},{1,33},{2,34},{3,35},{4,36},{5,37},{6,38},{7,39},{8,40},{9,... | collective-permute-start | bytes 2949128 | tf_op jit(solution)/shard_map/ppermute | solution.py:50
  63.9 24.8 %collective-permute-start.12 = (bf16[8,528,128]{2,1,0:T(8,128)(2,1)}, bf16[8,528,128]{2,1,0:T(8,128)(2,1)S(1)}, u32[]{:S(2)}, u32[]{:S(2)}) collective-permute-start(bf16[8,528,128]{2,1,0:T(8,128)(2,1)} %get-tuple-element.27.refs_5_), channel_id=1, source_target_pairs={{0,130},{1,131},{2,128},{3,129},{4,134},{5,135},{6,132},{7,133},{8... | collective-permute-start | bytes 3244040 | tf_op jit(solution)/shard_map/ppermute | solution.py:50
  64.7 1.0 copy-start.3
  65.7 25.1 %collective-permute-start.11 = (bf16[8,528,128]{2,1,0:T(8,128)(2,1)}, bf16[8,528,128]{2,1,0:T(8,128)(2,1)S(1)}, u32[]{:S(2)}, u32[]{:S(2)}) collective-permute-start(bf16[8,528,128]{2,1,0:T(8,128)(2,1)} %get-tuple-element.27.refs_5_), channel_id=1, source_target_pairs={{0,128},{1,129},{2,130},{3,131},{4,132},{5,133},{6,134},{7,135},{8... | collective-permute-start | bytes 3244040 | tf_op jit(solution)/shard_map/ppermute | solution.py:50
  66.7 1.0 copy-start.1
  67.7 13.5 %copy-start = (bf16[1,128,1536]{2,1,0:T(8,128)(2,1)S(1)}, bf16[1,128,1536]{2,1,0:T(8,128)(2,1)}, u32[]{:S(2)}) copy-start(bf16[1,128,1536]{2,1,0:T(8,128)(2,1)} %param.7) | copy-start | bytes 1179652
  67.7 1.3 copy-start.12
  75.6 0.7 copy-start.5
  76.4 21.7 %all-to-all-start.1 = ((bf16[8,160,128]{2,1,0:T(8,128)(2,1)}), bf16[8,160,128]{2,1,0:T(8,128)(2,1)}, u32[]{:S(2)}, u32[]{:S(2)}) async-start(bf16[8,160,128]{2,1,0:T(8,128)(2,1)} %copy-done.5), calls=%async_computation.1 | async-start | bytes 655360 | tf_op jit(solution)/shard_map/all_to_all | solution.py:363
  81.2 12.2 %collective-permute-start.16 = (bf16[16,1536]{1,0:T(8,128)(2,1)S(1)}, bf16[16,1536]{1,0:T(8,128)(2,1)S(1)}, u32[]{:S(2)}, u32[]{:S(2)}) collective-permute-start(bf16[16,1536]{1,0:T(8,128)(2,1)S(1)} %get-tuple-element.43), channel_id=1, source_target_pairs={{32,0},{64,32},{96,64},{128,96},{160,128},{192,160},{224,192},{33,... | collective-permute-start | bytes 147464 | tf_op jit(solution)/shard_map/ppermute | solution.py:365
  85.7 11.8 %collective-permute-start.15 = (bf16[16,1536]{1,0:T(8,128)(2,1)S(1)}, bf16[16,1536]{1,0:T(8,128)(2,1)S(1)}, u32[]{:S(2)}, u32[]{:S(2)}) collective-permute-start(bf16[16,1536]{1,0:T(8,128)(2,1)S(1)} %get-tuple-element.44), channel_id=1, source_target_pairs={{0,32},{32,64},{64,96},{96,128},{128,160},{160,192},{192,224},{1,3... | collective-permute-start | bytes 147464 | tf_op jit(solution)/shard_map/ppermute | solution.py:364
  93.4 0.6 copy-start.7
  97.5 0.6 copy-start.9
  98.1 24.5 %copy-start.2 = (bf16[8,528,128]{2,1,0:T(8,128)(2,1)S(1)}, bf16[8,528,128]{2,1,0:T(8,128)(2,1)}, u32[]{:S(2)}) copy-start(bf16[8,528,128]{2,1,0:T(8,128)(2,1)} %copy-done.1) | copy-start | bytes 3244036
  98.1 24.5 %copy-start.4 = (bf16[8,480,128]{2,1,0:T(8,128)(2,1)S(1)}, bf16[8,480,128]{2,1,0:T(8,128)(2,1)}, u32[]{:S(2)}) copy-start(bf16[8,480,128]{2,1,0:T(8,128)(2,1)} %copy-done.3) | copy-start | bytes 2949124
  98.1 24.5 %copy-start.6 = (bf16[31,1536]{1,0:T(8,128)(2,1)S(1)}, bf16[31,1536]{1,0:T(8,128)(2,1)}, u32[]{:S(2)}) copy-start(bf16[31,1536]{1,0:T(8,128)(2,1)} %taps_in.1) | copy-start | bytes 285700
  98.1 24.5 %copy-start.8 = (bf16[16,1536]{1,0:T(8,128)(2,1)S(1)}, bf16[16,1536]{1,0:T(8,128)(2,1)}, u32[]{:S(2)}) copy-start(bf16[16,1536]{1,0:T(8,128)(2,1)} %copy-done.7) | copy-start | bytes 147460
  98.1 24.5 %copy-start.10 = (bf16[16,1536]{1,0:T(8,128)(2,1)S(1)}, bf16[16,1536]{1,0:T(8,128)(2,1)}, u32[]{:S(2)}) copy-start(bf16[16,1536]{1,0:T(8,128)(2,1)} %copy-done.9) | copy-start | bytes 147460
  99.3 12.6 %collective-permute-start.17 = (bf16[4,480,128]{2,1,0:T(8,128)(2,1)S(1)}, bf16[4,480,128]{2,1,0:T(8,128)(2,1)S(1)}, u32[]{:S(2)}, u32[]{:S(2)}) collective-permute-start(bf16[4,480,128]{2,1,0:T(8,128)(2,1)S(1)} %get-tuple-element.39), channel_id=1, source_target_pairs={{0,96},{1,97},{2,98},{3,99},{4,100},{5,101},{6,102},{7,103},{8,104... | collective-permute-start | bytes 1474568 | tf_op jit(solution)/shard_map/ppermute | solution.py:50
  99.4 14.8 %collective-permute-start.19 = (bf16[4,528,128]{2,1,0:T(8,128)(2,1)S(1)}, bf16[4,528,128]{2,1,0:T(8,128)(2,1)S(1)}, u32[]{:S(2)}, u32[]{:S(2)}) collective-permute-start(bf16[4,528,128]{2,1,0:T(8,128)(2,1)S(1)} %get-tuple-element.41), channel_id=1, source_target_pairs={{0,130},{1,131},{2,128},{3,129},{4,134},{5,135},{6,132},{7,133},{8... | collective-permute-start | bytes 1622024 | tf_op jit(solution)/shard_map/ppermute | solution.py:50
  100.2 14.0 %collective-permute-start.18 = (bf16[4,480,128]{2,1,0:T(8,128)(2,1)S(1)}, bf16[4,480,128]{2,1,0:T(8,128)(2,1)S(1)}, u32[]{:S(2)}, u32[]{:S(2)}) collective-permute-start(bf16[4,480,128]{2,1,0:T(8,128)(2,1)S(1)} %get-tuple-element.40), channel_id=1, source_target_pairs={{0,32},{1,33},{2,34},{3,35},{4,36},{5,37},{6,38},{7,39},{8,40},{9,... | collective-permute-start | bytes 1474568 | tf_op jit(solution)/shard_map/ppermute | solution.py:50
  100.2 14.6 %collective-permute-start.20 = (bf16[4,528,128]{2,1,0:T(8,128)(2,1)S(1)}, bf16[4,528,128]{2,1,0:T(8,128)(2,1)S(1)}, u32[]{:S(2)}, u32[]{:S(2)}) collective-permute-start(bf16[4,528,128]{2,1,0:T(8,128)(2,1)S(1)} %get-tuple-element.42), channel_id=1, source_target_pairs={{0,128},{1,129},{2,130},{3,131},{4,132},{5,133},{6,134},{7,135},{8... | collective-permute-start | bytes 1622024 | tf_op jit(solution)/shard_map/ppermute | solution.py:50
  101.3 13.6 %collective-permute-start.21 = (bf16[8,480,128]{2,1,0:T(8,128)(2,1)}, bf16[8,480,128]{2,1,0:T(8,128)(2,1)S(1)}, u32[]{:S(2)}, u32[]{:S(2)}) collective-permute-start(bf16[8,480,128]{2,1,0:T(8,128)(2,1)} %collective-permute-done.9.beta_1.refs_1_), channel_id=1, source_target_pairs={{0,1},{1,0},{2,3},{3,2},{4,5},{5,4},{6,7},{7,6},{8,9},{9,8},{10,11... | collective-permute-start | bytes 2949128 | tf_op jit(solution)/shard_map/ppermute | solution.py:50
  111.9 4.5 %collective-permute-start.24 = (bf16[8,480,128]{2,1,0:T(8,128)(2,1)S(1)}, bf16[8,480,128]{2,1,0:T(8,128)(2,1)S(1)}, u32[]{:S(2)}, u32[]{:S(2)}) collective-permute-start(bf16[8,480,128]{2,1,0:T(8,128)(2,1)S(1)} %collective-permute-done.10.beta_3.refs_4_), channel_id=1, source_target_pairs={{0,1},{1,0},{2,3},{3,2},{4,5},{5,4},{6,7},{7,6},{8,9},{9,8},{10,11... | collective-permute-start | bytes 2949128 | tf_op jit(solution)/shard_map/ppermute | solution.py:50
  114.3 8.2 %collective-permute-start.25 = (bf16[8,528,128]{2,1,0:T(8,128)(2,1)S(1)}, bf16[8,528,128]{2,1,0:T(8,128)(2,1)S(1)}, u32[]{:S(2)}, u32[]{:S(2)}) collective-permute-start(bf16[8,528,128]{2,1,0:T(8,128)(2,1)S(1)} %collective-permute-done.11.gamma_1.refs_6_), channel_id=1, source_target_pairs={{0,1},{1,0},{2,3},{3,2},{4,5},{5,4},{6,7},{7,6},{8,9},{9,8},{10,11... | collective-permute-start | bytes 3244040 | tf_op jit(solution)/shard_map/ppermute | solution.py:50
  114.3 8.2 %collective-permute-start.28 = (bf16[8,528,128]{2,1,0:T(8,128)(2,1)S(1)}, bf16[8,528,128]{2,1,0:T(8,128)(2,1)S(1)}, u32[]{:S(2)}, u32[]{:S(2)}) collective-permute-start(bf16[8,528,128]{2,1,0:T(8,128)(2,1)S(1)} %collective-permute-done.12.gamma_3.refs_9_), channel_id=1, source_target_pairs={{0,1},{1,0},{2,3},{3,2},{4,5},{5,4},{6,7},{7,6},{8,9},{9,8},{10,11... | collective-permute-start | bytes 3244040 | tf_op jit(solution)/shard_map/ppermute | solution.py:50
  114.8 5.5 %collective-permute-start.22 = (bf16[4,480,128]{2,1,0:T(8,128)(2,1)S(1)}, bf16[4,480,128]{2,1,0:T(8,128)(2,1)S(1)}, u32[]{:S(2)}, u32[]{:S(2)}) collective-permute-start(bf16[4,480,128]{2,1,0:T(8,128)(2,1)S(1)} %collective-permute-done.17.refs_2_), channel_id=1, source_target_pairs={{0,1},{1,0},{2,3},{3,2},{4,5},{5,4},{6,7},{7,6},{8,9},{9,8},{10,11... | collective-permute-start | bytes 1474568 | tf_op jit(solution)/shard_map/ppermute | solution.py:50
  114.9 7.6 %collective-permute-start.26 = (bf16[4,528,128]{2,1,0:T(8,128)(2,1)S(1)}, bf16[4,528,128]{2,1,0:T(8,128)(2,1)S(1)}, u32[]{:S(2)}, u32[]{:S(2)}) collective-permute-start(bf16[4,528,128]{2,1,0:T(8,128)(2,1)S(1)} %collective-permute-done.19.refs_7_), channel_id=1, source_target_pairs={{0,1},{1,0},{2,3},{3,2},{4,5},{5,4},{6,7},{7,6},{8,9},{9,8},{10,11... | collective-permute-start | bytes 1622024 | tf_op jit(solution)/shard_map/ppermute | solution.py:50
  116.5 6.1 %collective-permute-start.27 = (bf16[4,528,128]{2,1,0:T(8,128)(2,1)S(1)}, bf16[4,528,128]{2,1,0:T(8,128)(2,1)S(1)}, u32[]{:S(2)}, u32[]{:S(2)}) collective-permute-start(bf16[4,528,128]{2,1,0:T(8,128)(2,1)S(1)} %collective-permute-done.20.refs_8_), channel_id=1, source_target_pairs={{0,1},{1,0},{2,3},{3,2},{4,5},{5,4},{6,7},{7,6},{8,9},{9,8},{10,11... | collective-permute-start | bytes 1622024 | tf_op jit(solution)/shard_map/ppermute | solution.py:50
  120.3 2.2 %collective-permute-start.23 = (bf16[4,480,128]{2,1,0:T(8,128)(2,1)S(1)}, bf16[4,480,128]{2,1,0:T(8,128)(2,1)S(1)}, u32[]{:S(2)}, u32[]{:S(2)}) collective-permute-start(bf16[4,480,128]{2,1,0:T(8,128)(2,1)S(1)} %collective-permute-done.18.refs_3_), channel_id=1, source_target_pairs={{0,1},{1,0},{2,3},{3,2},{4,5},{5,4},{6,7},{7,6},{8,9},{9,8},{10,11... | collective-permute-start | bytes 1474568 | tf_op jit(solution)/shard_map/ppermute | solution.py:50

commit v2 on v1

--- a/solution.py
+++ b/solution.py
@@ -96,10 +96,10 @@
 
 
 BETA, GAMMA = 480, 528
-NEAR = BETA // 2 + 288
-
-
-def pack_kernel(x, w_qkv, w_out, w_glu, w_conv, beta, gam, normed, held, rows, sems):
+NEAR = BETA // 2 + 224
+
+
+def pack_kernel(x, w_qkv, w_out, w_glu, w_conv, beta, gam, normed, held, head, rows, sems):
     ctx, y, a, _, _, core = whereabouts()
     glu, conv = core * 12, core * 6
     copies = [
@@ -117,7 +117,7 @@
         copies.append((w_glu.at[:, columns(glu + 8 + 2 * a + j)], gam.at[144 + 96 * j : 240 + 96 * j, :]))
         copies.append((w_conv.at[48:96, columns(conv + 2 * a + j)], gam.at[336 + 48 * j : 384 + 48 * j, :]))
     wait = run_copies(copies, sems)
-    beta[240:528, :] = jnp.zeros((288, LANES), BF16)
+    beta[432:464, :] = jnp.zeros((32, LANES), BF16)
     wait()
     for j in range(HEADS):
 
@@ -125,8 +125,12 @@
         def _():
             for part in range(3):
                 first = part * 768 + DH * j
-                beta[240 + 96 * part : 336 + 96 * part, 0:DH] = held[:, first : first + DH]
-
+                head[:, DH * part : DH * (part + 1)] = held[:, first : first + DH]
+
+    beta[240:336, :] = head[:, 0:128]
+    beta[336:432, :] = head[:, 128:256]
+    for g in range(3):
+        beta[432:464, 32 * g : 32 * (g + 1)] = head[32 * g : 32 * (g + 1), 256:288]
     normed[...] = norm_rows(rows[...].astype(F32)).astype(BF16)
 
 
@@ -141,9 +145,13 @@
         for side in range(2):
             first = NEAR * side
             beta[at, 240 * side : 240 * (side + 1), :] = ref[first : first + 240, :]
-            for part in range(3):
-                start = first + 240 + 96 * part
-                w[at, side, :, LANES * part : LANES * (part + 1)] = ref[start : start + 96, :]
+            w[at, side, :, 0:128] = ref[first + 240 : first + 336, :]
+            w[at, side, :, 128:256] = ref[first + 336 : first + 432, :]
+            for g in range(3):
+                w[at, side, 32 * g : 32 * (g + 1), 256:288] = ref[
+                    first + 432 : first + 464, 32 * g : 32 * (g + 1)
+                ]
+            w[at, side, :, 288:384] = jnp.zeros((96, 96), BF16)
 
     near(low, z ^ 4)
     gam[z ^ 4] = high[...]
@@ -156,12 +164,14 @@
 def attend_kernel(length, x, w, out, q, k, v, att):
     att[0:HALO, :] = jnp.zeros((HALO, LANES), BF16)
     att[SEQ + HALO : SEQ + 2 * HALO, :] = jnp.zeros((HALO, LANES), BF16)
+    for ref in (q, k, v):
+        ref[:, DH:LANES] = jnp.zeros((SEQ, LANES - DH), BF16)
     mat = w[...].reshape(D, 3 * LANES)
     for i in range(4):
         rows = slice(256 * i, 256 * (i + 1))
         made = jnp.dot(x[2 * i : 2 * i + 2].reshape(256, D), mat, preferred_element_type=F32).astype(BF16)
         for part, ref in enumerate((q, k, v)):
-            ref[rows, :] = made[:, LANES * part : LANES * (part + 1)]
+            ref[rows, 0:DH] = made[:, DH * part : DH * (part + 1)]
     valid = lax.broadcasted_iota(jnp.int32, (1, SEQ), 1) < length[0]
     keys, values = k[...], v[...]
     for i in range(HEADS):
@@ -195,7 +205,7 @@
 
 def middle_kernel(length, att_in, frames_in, before_in, behind_in, taps_in, *refs):
     pieces = refs[0:20]
-    out, att, frames, taps, w_out, w, w_conv, ext, summed, own_sems, out_sems, glu_sems, conv_sems = refs[20:]
+    out, att, frames, taps, heads, rows, w_out, w, w_conv, ext, summed, own_sems, out_sems, glu_sems, conv_sems = refs[20:]
     own_wait = run_copies(
         [
             (att_in, att), (before_in, frames.at[0:HALO]), (frames_in, frames.at[HALO : HALO + ROWS]),
@@ -228,49 +238,61 @@
             copies.append((ref.at[:, 0:48, :], w_out.at[z, h ^ (i >> 1), :, columns(at * 6 + 4 + (a ^ (i & 1)))]))
     out_wait = run_copies(copies, out_sems)
     whole, low, high = slice(0, 96), slice(0, 48), slice(48, 96)
-    for first, at in owners:
-        for i, z, ref in halves(pieces[first : first + 5]):
-            for side in range(2):
-                start = 240 * side + 48
-                glu_copy(ref.at[:, start : start + 96, :], z, whole, side, at * 12 + (y ^ i))
-    for first, at in owners:
-        for i, z, ref in halves(pieces[first : first + 5]):
-            for side in range(2):
-                start = 240 * side + 144
-                glu_copy(ref.at[:, start : start + 48, :], z, low, side, at * 12 + 4 + (y ^ i))
-        for i, z, ref in halves(pieces[first + 5 : first + 10]):
-            block = at * 12 + 4 + 2 * (a ^ (i & 1))
-            for j in range(2):
-                start = 48 + 48 * j
-                glu_copy(ref.at[:, start : start + 48, :], z, high, h ^ (i >> 1), block + j)
-    for first, at in owners:
-        for i, z, ref in halves(pieces[first + 5 : first + 10]):
-            block = at * 12 + 8 + 2 * (a ^ (i & 1))
-            for j in range(2):
-                start = 144 + 96 * j
-                glu_copy(ref.at[:, start : start + 96, :], z, whole, h ^ (i >> 1), block + j)
-
-    for first, at in owners:
-        for i, z, ref in halves(pieces[first : first + 5]):
-            for side in range(2):
-                start = 240 * side + 192
-                conv_copy(ref.at[:, start : start + 48, :], z, low, side, at * 6 + (y ^ i))
-        for i, z, ref in halves(pieces[first + 5 : first + 10]):
-            there = a ^ (i & 1)
-            for j in range(2):
-                start = 336 + 48 * j
-                conv_copy(ref.at[:, start : start + 48, :], z, high, h ^ (i >> 1), at * 6 + 2 * there + j)
-            conv_copy(ref.at[:, 432:528, :], z, whole, h ^ (i >> 1), at * 6 + 4 + there)
-
+
+    def start_beta():
+        for first, at in owners:
+            for i, z, ref in halves(pieces[first : first + 5]):
+                for side in range(2):
+                    start = 240 * side + 48
+                    glu_copy(ref.at[:, start : start + 96, :], z, whole, side, at * 12 + (y ^ i))
+
+    def start_mixed():
+        for first, at in owners:
+            for i, z, ref in halves(pieces[first : first + 5]):
+                for side in range(2):
+                    start = 240 * side + 144
+                    glu_copy(ref.at[:, start : start + 48, :], z, low, side, at * 12 + 4 + (y ^ i))
+            for i, z, ref in halves(pieces[first + 5 : first + 10]):
+                block = at * 12 + 4 + 2 * (a ^ (i & 1))
+                for j in range(2):
+                    start = 48 + 48 * j
+                    glu_copy(ref.at[:, start : start + 48, :], z, high, h ^ (i >> 1), block + j)
+
+    def start_gamma():
+        for first, at in owners:
+            for i, z, ref in halves(pieces[first + 5 : first + 10]):
+                block = at * 12 + 8 + 2 * (a ^ (i & 1))
+                for j in range(2):
+                    start = 144 + 96 * j
+                    glu_copy(ref.at[:, start : start + 96, :], z, whole, h ^ (i >> 1), block + j)
+
+    def start_conv():
+        for first, at in owners:
+            for i, z, ref in halves(pieces[first : first + 5]):
+                for side in range(2):
+                    start = 240 * side + 192
+                    conv_copy(ref.at[:, start : start + 48, :], z, low, side, at * 6 + (y ^ i))
+            for i, z, ref in halves(pieces[first + 5 : first + 10]):
+                there = a ^ (i & 1)
+                for j in range(2):
+                    start = 336 + 48 * j
+                    conv_copy(ref.at[:, start : start + 48, :], z, high, h ^ (i >> 1), at * 6 + 2 * there + j)
+                conv_copy(ref.at[:, 432:528, :], z, whole, h ^ (i >> 1), at * 6 + 4 + there)
+
+    start_beta()
+    own_wait()
+    for head in range(HEADS):
+        heads[:, DH * head : DH * (head + 1)] = att[head, :, 0:DH]
     out_wait()
-    own_wait()
-    total = frames[...].astype(F32)
-    for head in range(HEADS):
-        mat = w_out[head].reshape(DH, D)
-        total = total + jnp.dot(att[head][:, 0:DH], mat, preferred_element_type=F32)
-    total = total.astype(BF16)
-    mixed = total[HALO : HALO + ROWS]
-    rows = norm_rows(total.astype(F32)).astype(BF16)
+    for n in range(6):
+        cols = slice(256 * n, 256 * (n + 1))
+        mat = w_out[:, :, :, cols].reshape(HEADS * DH, 256)
+        total = frames[:, cols].astype(F32) + jnp.dot(heads[...], mat, preferred_element_type=F32)
+        frames[:, cols] = total.astype(BF16)
+    start_mixed()
+    for i in range(WIDE // 32):
+        part = slice(32 * i, 32 * (i + 1))
+        rows[part, :] = norm_rows(frames[part, :].astype(F32)).astype(BF16)
 
     position = lax.axis_index("ctx") * ROWS - HALO + lax.broadcasted_iota(jnp.int32, (WIDE, 1), 0)
     valid = (position >= 0) & (position < length[0])
@@ -280,23 +302,35 @@
         mats = [
             w[:, :, :, at + 256 * n : at + 256 * (n + 1)].reshape(D, 256) for at in (0, D)
         ]
-        value, gate = [jnp.dot(rows, mat, preferred_element_type=F32) for mat in mats]
+        value, gate = [jnp.dot(rows[...], mat, preferred_element_type=F32) for mat in mats]
         gated = value * jax.nn.sigmoid(gate)
         ext[:, 256 * n : 256 * (n + 1)] = jnp.where(valid, gated, 0.0).astype(BF16).astype(F32)
+        if n == 0:
+            start_gamma()
+        if n == 2:
+            start_conv()
         for m in (2 * n, 2 * n + 1):
             cols = slice(LANES * m, LANES * (m + 1))
             total = jnp.zeros((ROWS, LANES), F32)
             tap_rows = taps[:, cols].astype(F32)
-            for j in range(TAPS):
-                total = total + tap_rows[j : j + 1, :] * ext[j + 1 : j + 1 + ROWS, cols]
+            for r in range(8):
+                moved = ext[r : r + ROWS + 24, cols]
+                for k in range(4):
+                    j = 8 * k + r - 1
+                    if 0 <= j < TAPS:
+                        total = total + tap_rows[j : j + 1, :] * moved[8 * k : 8 * k + ROWS]
             summed[:, cols] = total
-    normed = norm_rows(summed[...])
-    activated = (normed * jax.nn.sigmoid(normed)).astype(BF16)
+    for i in range(ROWS // 16):
+        part = slice(16 * i, 16 * (i + 1))
+        normed = norm_rows(summed[part, :])
+        rows[part, :] = (normed * jax.nn.sigmoid(normed)).astype(BF16)
     pltpu.make_async_copy(w_conv, w_conv, conv_sems.at[0]).wait()
     for n in range(6):
         cols = slice(256 * n, 256 * (n + 1))
         mat = w_conv[:, :, :, cols].reshape(D, 256)
-        total = mixed[:, cols].astype(F32) + jnp.dot(activated, mat, preferred_element_type=F32)
+        total = frames[HALO : HALO + ROWS, cols].astype(F32) + jnp.dot(
+            rows[0:ROWS, :], mat, preferred_element_type=F32
+        )
         out[:, cols] = total.astype(BF16)
 
 
@@ -320,7 +354,8 @@
         in_specs=[ANY] * 5,
         out_specs=(VM,) * 3,
         scratch_shapes=[
-            pltpu.VMEM((96, 2304), BF16), pltpu.VMEM((ROWS, D), BF16), pltpu.SemaphoreType.DMA((14,))
+            pltpu.VMEM((96, 2304), BF16), pltpu.VMEM((96, 384), BF16), pltpu.VMEM((ROWS, D), BF16),
+            pltpu.SemaphoreType.DMA((14,)),
         ],
         compiler_params=params(),
     )(frame_rows, w_qkv, w_out, w_glu, w_conv_out)
@@ -394,6 +429,8 @@
             pltpu.VMEM((8, WIDE, LANES), BF16),
             pltpu.VMEM((WIDE, D), BF16),
             pltpu.VMEM((TAPS, D), BF16),
+            pltpu.VMEM((WIDE, HEADS * DH), BF16),
+            pltpu.VMEM((WIDE, D), BF16),
             pltpu.VMEM((8, 2, 48, D), BF16),
             pltpu.VMEM((8, 2, 96, 2 * D), BF16),
             pltpu.VMEM((8, 2, 96, D), BF16),

time: 137 us -> 135 us (0.985)
  waiting for transfers between devices: 51.2 us -> 49.3 us
    ppermute x27, waiting for transfers between devices: 45.2 us -> 43.4 us  [send(): return lax.ppermute(value, AXES, moves)]
where the time goes in v2:
time: 135 us; the launch traced here: 134 us
  waiting for transfers between devices  49.3 us (37%)
  starting transfers between devices  48.7 us (36%)
  Pallas kernels  25.7 us (19%)
  local copies, waits for them, and re-layouts  9.29 us (7%)
    ppermute x27, waiting for transfers between devices, send(): return lax.ppermute(value, AXES, moves)  43.4 us
    ppermute x27, starting transfers between devices, send(): return lax.ppermute(value, AXES, moves)  32.2 us
    pallas_call x1, Pallas kernels, per_device(): pl.pallas_call(middle_kernel, out_shape=shape(ROWS, D), in_specs=[SM] + [...  13.5 us
    pallas_call x1, Pallas kernels, per_device(): pl.pallas_call(attend_kernel, out_shape=shape(8, WIDE, LANES), in_specs=[...  6.75 us
    unnamed x30, local copies, waits for them, and re-layouts  6.32 us
    all_to_all x1, starting transfers between devices, per_device(): lax.all_to_all(jnp.broadcast_to(normed[None], (8, ROWS, D)), 'ctx', 0, 0)  5.65 us
    all_to_all x1, starting transfers between devices, per_device(): att = lax.all_to_all(att, 'ctx', 0, 0)  4.67 us
    ppermute x1, starting transfers between devices, per_device(): frames_behind = lax.ppermute(halo[:HALO], 'ctx', down)  4.3 us
  transfers between devices with their start and end apart: 31, of which 15 were waited for; matrix products, arithmetic and copies ran while one was open for 2% of the time, Pallas kernels for 6%

profile of v2, /device:TPU:3, one launch (start us, length us, event | category | flops | bytes accessed | tf_op | source)
XLA Modules:
  0.0 134.1 jit_solution(15410397484626204372)
XLA Ops:
  0.0 2.4 %shard_map.73 = (bf16[464,128]{1,0:T(8,128)(2,1)}, bf16[528,128]{1,0:T(8,128)(2,1)}, bf16[128,1536]{1,0:T(8,128)(2,1)}) custom-call(bf16[128,1536]{1,0:T(8,128)(2,1)} %bitcast.2, bf16[96,2304]{1,0:T(8,128)(2,1)} %w_qkv.1, bf16[48,1536]{1,0:T(8,128)(2,1)} %w_out.1, bf16[96,3072]{1,0:T(8,128)(2,1)} %w_glu.1, bf16[96,1536]{1,0:T(8,128)(2,1)} %w_conv.1), custom_call_target="tpu_custom_call" | custom-call | tf_op jit(solution)/shard_map/pallas_call | solution.py:351
  2.4 1.9 %collective-permute-start = (bf16[464,128]{1,0:T(8,128)(2,1)}, bf16[464,128]{1,0:T(8,128)(2,1)S(1)}, u32[]{:S(2)}, u32[]{:S(2)}) collective-permute-start(bf16[464,128]{1,0:T(8,128)(2,1)} %get-tuple-element.24), channel_id=1, source_target_pairs={{0,2},{1,3},{2,0},{3,1},{4,6},{5,7},{6,4},{7,5},{8,10},{9,11},{10,... | collective-permute-start | bytes 356360 | tf_op jit(solution)/shard_map/ppermute | solution.py:50
  4.4 2.9 %broadcast_in_dim.4 = bf16[8,128,1536]{2,1,0:T(8,128)(2,1)} broadcast(bf16[128,1536]{1,0:T(8,128)(2,1)} %get-tuple-element.28), dimensions={1,2} | broadcast | bytes 3538944 | tf_op jit(solution)/shard_map/broadcast_in_dim | solution.py:363
  7.3 5.6 %all-to-all-start = ((bf16[8,128,1536]{2,1,0:T(8,128)(2,1)}), bf16[8,128,1536]{2,1,0:T(8,128)(2,1)}, u32[]{:S(2)}, u32[]{:S(2)}) async-start(bf16[8,128,1536]{2,1,0:T(8,128)(2,1)} %broadcast_in_dim.4), calls=%async_computation | async-start | bytes 6291456 | tf_op jit(solution)/shard_map/all_to_all | solution.py:363
  13.0 1.7 %collective-permute-start.1 = (bf16[1456,128]{1,0:T(8,128)(2,1)S(1)}, bf16[1456,128]{1,0:T(8,128)(2,1)S(1)}, u32[]{:S(2)}, u32[]{:S(2)}) collective-permute-start(bf16[1456,128]{1,0:T(8,128)(2,1)S(1)} %pad_maximum_fusion.refs_0_), channel_id=1, source_target_pairs={{0,4},{1,5},{2,6},{3,7},{4,8},{5,9},{6,10},{7,11},{8,12},{9,13},{1... | collective-permute-start | bytes 1118216 | tf_op jit(solution)/shard_map/ppermute | solution.py:50
  14.8 4.0 %collective-permute-start.4 = (bf16[1456,128]{1,0:T(8,128)(2,1)S(1)}, bf16[1456,128]{1,0:T(8,128)(2,1)S(1)}, u32[]{:S(2)}, u32[]{:S(2)}) collective-permute-start(bf16[1456,128]{1,0:T(8,128)(2,1)S(1)} %pad_maximum_fusion.refs_0_), channel_id=1, source_target_pairs={{0,28},{1,29},{2,30},{3,31},{4,0},{5,1},{6,2},{7,3},{8,4},{9,5},{1... | collective-permute-start | bytes 1118216 | tf_op jit(solution)/shard_map/ppermute | solution.py:50
  18.8 7.6 %collective-permute-done.1.refs_1_ = bf16[1456,128]{1,0:T(8,128)(2,1)S(1)} collective-permute-done((bf16[1456,128]{1,0:T(8,128)(2,1)S(1)}, bf16[1456,128]{1,0:T(8,128)(2,1)S(1)}, u32[]{:S(2)}, u32[]{:S(2)}) %collective-permute-start.1) | collective-permute-done | bytes 372768 | tf_op jit(solution)/shard_map/ppermute | solution.py:50
  26.4 2.7 %collective-permute-start.5 = (bf16[1456,128]{1,0:T(8,128)(2,1)S(1)}, bf16[1456,128]{1,0:T(8,128)(2,1)S(1)}, u32[]{:S(2)}, u32[]{:S(2)}) collective-permute-start(bf16[1456,128]{1,0:T(8,128)(2,1)S(1)} %collective-permute-done.4.refs_4_), channel_id=1, source_target_pairs={{0,28},{1,29},{2,30},{3,31},{4,0},{5,1},{6,2},{7,3},{8,4},{9,5},{1... | collective-permute-start | bytes 1118216 | tf_op jit(solution)/shard_map/ppermute | solution.py:50
  29.1 6.9 %collective-permute-done.2.refs_2_ = bf16[1456,128]{1,0:T(8,128)(2,1)S(1)} collective-permute-done((bf16[1456,128]{1,0:T(8,128)(2,1)S(1)}, bf16[1456,128]{1,0:T(8,128)(2,1)S(1)}, u32[]{:S(2)}, u32[]{:S(2)}) %collective-permute-start.2) | collective-permute-done | bytes 372768 | tf_op jit(solution)/shard_map/ppermute | solution.py:50
  36.0 2.7 %collective-permute-start.6 = (bf16[1456,128]{1,0:T(8,128)(2,1)S(1)}, bf16[1456,128]{1,0:T(8,128)(2,1)S(1)}, u32[]{:S(2)}, u32[]{:S(2)}) collective-permute-start(bf16[1456,128]{1,0:T(8,128)(2,1)S(1)} %collective-permute-done.5.refs_5_), channel_id=1, source_target_pairs={{0,28},{1,29},{2,30},{3,31},{4,0},{5,1},{6,2},{7,3},{8,4},{9,5},{1... | collective-permute-start | bytes 1118216 | tf_op jit(solution)/shard_map/ppermute | solution.py:50
  38.7 6.1 %collective-permute-done.3.refs_3_ = bf16[1456,128]{1,0:T(8,128)(2,1)S(1)} collective-permute-done((bf16[1456,128]{1,0:T(8,128)(2,1)S(1)}, bf16[1456,128]{1,0:T(8,128)(2,1)S(1)}, u32[]{:S(2)}, u32[]{:S(2)}) %collective-permute-start.3) | collective-permute-done | bytes 372768 | tf_op jit(solution)/shard_map/ppermute | solution.py:50
  44.9 2.7 %collective-permute-start.8 = (bf16[528,128]{1,0:T(8,128)(2,1)S(1)}, bf16[528,128]{1,0:T(8,128)(2,1)S(1)}, u32[]{:S(2)}, u32[]{:S(2)}) collective-permute-start(bf16[528,128]{1,0:T(8,128)(2,1)S(1)} %slice.17), channel_id=1, source_target_pairs={{0,28},{1,29},{2,30},{3,31},{4,0},{5,1},{6,2},{7,3},{8,4},{9,5},{1... | collective-permute-start | bytes 405512 | tf_op jit(solution)/shard_map/ppermute | solution.py:50
  47.6 2.0 %collective-permute-done.8.refs_8_ = bf16[528,128]{1,0:T(8,128)(2,1)S(1)} collective-permute-done((bf16[528,128]{1,0:T(8,128)(2,1)S(1)}, bf16[528,128]{1,0:T(8,128)(2,1)S(1)}, u32[]{:S(2)}, u32[]{:S(2)}) %collective-permute-start.8) | collective-permute-done | bytes 135200 | tf_op jit(solution)/shard_map/ppermute | solution.py:50
  49.6 1.4 %collective-permute-done.7.refs_7_ = bf16[928,128]{1,0:T(8,128)(2,1)S(1)} collective-permute-done((bf16[928,128]{1,0:T(8,128)(2,1)S(1)}, bf16[928,128]{1,0:T(8,128)(2,1)S(1)}, u32[]{:S(2)}, u32[]{:S(2)}) %collective-permute-start.7) | collective-permute-done | bytes 237600 | tf_op jit(solution)/shard_map/ppermute | solution.py:50
  51.0 1.8 %shard_map.74 = (bf16[8,2,96,384]{3,2,1,0:T(8,128)(2,1)S(1)}, bf16[8,480,128]{2,1,0:T(8,128)(2,1)}, bf16[8,528,128]{2,1,0:T(8,128)(2,1)}) custom-call(bf16[1456,128]{1,0:T(8,128)(2,1)S(1)} %pad_maximum_fusion.refs_0_, bf16[1456,128]{1,0:T(8,128)(2,1)S(1)} %collective-permute-done.1.refs_1_, bf16[1456,128]{1,0:T(8,128)(2,1)S(1)} %collective-permute-done.2.refs_2_, ...), custom_call_target="tpu_custom_call" | custom-call | tf_op jit(solution)/shard_map/pallas_call | solution.py:368
  52.8 1.0 copy-done.11
  53.9 4.7 %collective-permute-start.14 = (bf16[8,528,128]{2,1,0:T(8,128)(2,1)}, bf16[8,528,128]{2,1,0:T(8,128)(2,1)S(1)}, u32[]{:S(2)}, u32[]{:S(2)}) collective-permute-start(bf16[8,528,128]{2,1,0:T(8,128)(2,1)} %get-tuple-element.27.refs_5_), channel_id=1, source_target_pairs={{0,1},{1,0},{2,3},{3,2},{4,5},{5,4},{6,7},{7,6},{8,9},{9,8},{10,11... | collective-permute-start | bytes 3244040 | tf_op jit(solution)/shard_map/ppermute | solution.py:50
  59.2 2.5 %collective-permute-start.10 = (bf16[8,480,128]{2,1,0:T(8,128)(2,1)}, bf16[8,480,128]{2,1,0:T(8,128)(2,1)S(1)}, u32[]{:S(2)}, u32[]{:S(2)}) collective-permute-start(bf16[8,480,128]{2,1,0:T(8,128)(2,1)} %get-tuple-element.26.refs_0_), channel_id=1, source_target_pairs={{0,96},{1,97},{2,98},{3,99},{4,100},{5,101},{6,102},{7,103},{8,104... | collective-permute-start | bytes 2949128 | tf_op jit(solution)/shard_map/ppermute | solution.py:50
  61.8 0.8 collective-permute-done.13.refs_10_
  62.5 1.0 copy-done.3
  63.5 1.0 collective-permute-start.11
  64.5 1.0 copy-done.1
  65.5 1.3 copy-done.12
  66.8 6.7 %shard_map.75 = bf16[8,160,128]{2,1,0:T(8,128)(2,1)S(1)} custom-call(s32[1]{0:T(128)S(6)} %copy.8.length, bf16[8,128,1536]{2,1,0:T(8,128)(2,1)} %all-to-all-done.x, bf16[8,2,96,384]{3,2,1,0:T(8,128)(2,1)S(1)} %copy-done.12), custom_call_target="tpu_custom_call" | custom-call | flops 20000000000 | bytes 1048576 | tf_op jit(solution)/shard_map/pallas_call | solution.py:380
  73.6 0.7 copy-done.5
  74.3 4.7 %all-to-all-start.1 = ((bf16[8,160,128]{2,1,0:T(8,128)(2,1)}), bf16[8,160,128]{2,1,0:T(8,128)(2,1)}, u32[]{:S(2)}, u32[]{:S(2)}) async-start(bf16[8,160,128]{2,1,0:T(8,128)(2,1)} %copy-done.5), calls=%async_computation.1 | async-start | bytes 655360 | tf_op jit(solution)/shard_map/all_to_all | solution.py:398
  79.0 4.3 %collective-permute-start.16 = (bf16[16,1536]{1,0:T(8,128)(2,1)S(1)}, bf16[16,1536]{1,0:T(8,128)(2,1)S(1)}, u32[]{:S(2)}, u32[]{:S(2)}) collective-permute-start(bf16[16,1536]{1,0:T(8,128)(2,1)S(1)} %get-tuple-element.43), channel_id=1, source_target_pairs={{32,0},{64,32},{96,64},{128,96},{160,128},{192,160},{224,192},{33,... | collective-permute-start | bytes 147464 | tf_op jit(solution)/shard_map/ppermute | solution.py:400
  83.5 1.9 %collective-permute-start.15 = (bf16[16,1536]{1,0:T(8,128)(2,1)S(1)}, bf16[16,1536]{1,0:T(8,128)(2,1)S(1)}, u32[]{:S(2)}, u32[]{:S(2)}) collective-permute-start(bf16[16,1536]{1,0:T(8,128)(2,1)S(1)} %get-tuple-element.44), channel_id=1, source_target_pairs={{0,32},{32,64},{64,96},{96,128},{128,160},{160,192},{192,224},{1,3... | collective-permute-start | bytes 147464 | tf_op jit(solution)/shard_map/ppermute | solution.py:399
  85.5 1.1 collective-permute-done.12.gamma_3.refs_9_
  86.5 2.3 %collective-permute-done.11.gamma_1.refs_6_ = bf16[8,528,128]{2,1,0:T(8,128)(2,1)S(1)} collective-permute-done((bf16[8,528,128]{2,1,0:T(8,128)(2,1)}, bf16[8,528,128]{2,1,0:T(8,128)(2,1)S(1)}, u32[]{:S(2)}, u32[]{:S(2)}) %collective-permute-start.11) | collective-permute-done | bytes 1081376 | tf_op jit(solution)/shard_map/ppermute | solution.py:50
  88.8 2.7 %collective-permute-done.16.behind_in = bf16[16,1536]{1,0:T(8,128)(2,1)S(1)} collective-permute-done((bf16[16,1536]{1,0:T(8,128)(2,1)S(1)}, bf16[16,1536]{1,0:T(8,128)(2,1)S(1)}, u32[]{:S(2)}, u32[]{:S(2)}) %collective-permute-start.16) | collective-permute-done | bytes 49184 | tf_op jit(solution)/shard_map/ppermute | solution.py:400
  91.5 0.6 copy-done.7
  92.1 3.2 %collective-permute-done.15.before_in = bf16[16,1536]{1,0:T(8,128)(2,1)S(1)} collective-permute-done((bf16[16,1536]{1,0:T(8,128)(2,1)S(1)}, bf16[16,1536]{1,0:T(8,128)(2,1)S(1)}, u32[]{:S(2)}, u32[]{:S(2)}) %collective-permute-start.15) | collective-permute-done | bytes 49184 | tf_op jit(solution)/shard_map/ppermute | solution.py:399
  95.3 0.6 copy-done.9
  96.0 1.2 shard_map.76
  97.3 0.7 collective-permute-start.19
  98.0 1.0 collective-permute-start.20
  99.0 2.2 %collective-permute-start.21 = (bf16[8,480,128]{2,1,0:T(8,128)(2,1)}, bf16[8,480,128]{2,1,0:T(8,128)(2,1)S(1)}, u32[]{:S(2)}, u32[]{:S(2)}) collective-permute-start(bf16[8,480,128]{2,1,0:T(8,128)(2,1)} %collective-permute-done.9.beta_1.refs_1_), channel_id=1, source_target_pairs={{0,1},{1,0},{2,3},{3,2},{4,5},{5,4},{6,7},{7,6},{8,9},{9,8},{10,11... | collective-permute-start | bytes 2949128 | tf_op jit(solution)/shard_map/ppermute | solution.py:50
  101.2 8.6 %collective-permute-done.17.refs_2_ = bf16[4,480,128]{2,1,0:T(8,128)(2,1)S(1)} collective-permute-done((bf16[4,480,128]{2,1,0:T(8,128)(2,1)S(1)}, bf16[4,480,128]{2,1,0:T(8,128)(2,1)S(1)}, u32[]{:S(2)}, u32[]{:S(2)}) %collective-permute-start.17) | collective-permute-done | bytes 491552 | tf_op jit(solution)/shard_map/ppermute | solution.py:50
  109.8 2.3 %collective-permute-start.24 = (bf16[8,480,128]{2,1,0:T(8,128)(2,1)S(1)}, bf16[8,480,128]{2,1,0:T(8,128)(2,1)S(1)}, u32[]{:S(2)}, u32[]{:S(2)}) collective-permute-start(bf16[8,480,128]{2,1,0:T(8,128)(2,1)S(1)} %collective-permute-done.10.beta_3.refs_4_), channel_id=1, source_target_pairs={{0,1},{1,0},{2,3},{3,2},{4,5},{5,4},{6,7},{7,6},{8,9},{9,8},{10,11... | collective-permute-start | bytes 2949128 | tf_op jit(solution)/shard_map/ppermute | solution.py:50
  112.1 0.5 collective-permute-start.28
  112.7 0.4 collective-permute-start.26
  113.2 1.2 collective-permute-done.24.refs_14_
  114.3 0.4 collective-permute-start.27
  114.7 3.4 %collective-permute-done.22.refs_12_ = bf16[4,480,128]{2,1,0:T(8,128)(2,1)S(1)} collective-permute-done((bf16[4,480,128]{2,1,0:T(8,128)(2,1)S(1)}, bf16[4,480,128]{2,1,0:T(8,128)(2,1)S(1)}, u32[]{:S(2)}, u32[]{:S(2)}) %collective-permute-start.22) | collective-permute-done | bytes 491552 | tf_op jit(solution)/shard_map/ppermute | solution.py:50
  118.1 0.4 collective-permute-start.23
  118.5 1.9 %collective-permute-done.23.refs_13_ = bf16[4,480,128]{2,1,0:T(8,128)(2,1)S(1)} collective-permute-done((bf16[4,480,128]{2,1,0:T(8,128)(2,1)S(1)}, bf16[4,480,128]{2,1,0:T(8,128)(2,1)S(1)}, u32[]{:S(2)}, u32[]{:S(2)}) %collective-permute-start.23) | collective-permute-done | bytes 491552 | tf_op jit(solution)/shard_map/ppermute | solution.py:50
  120.4 13.5 %shard_map.77 = bf16[128,1536]{1,0:T(8,128)(2,1)} custom-call(s32[1]{0:T(128)S(6)} %copy.8.length, bf16[8,160,128]{2,1,0:T(8,128)(2,1)} %all-to-all-done.1.att_in, bf16[128,1536]{1,0:T(8,128)(2,1)S(1)} %bitcast.4, bf16[16,1536]{1,0:T(8,128)(2,1)S(1)} %copy-done.10, bf16[16,1536]{1,0:T(8,128)(2,1)S(1)} %copy-done.8, bf16[31,1536]{1,0:T(8,128)(2,1)S(1)} %copy-done.6, ...), custom_call_target="tpu_custom_call" | custom-call | tf_op jit(solution)/shard_map/pallas_call | solution.py:423
  (55 shorter events, 0.7 us)
Async XLA Ops:
  2.4 10.5 %collective-permute-start = (bf16[464,128]{1,0:T(8,128)(2,1)}, bf16[464,128]{1,0:T(8,128)(2,1)S(1)}, u32[]{:S(2)}, u32[]{:S(2)}) collective-permute-start(bf16[464,128]{1,0:T(8,128)(2,1)} %get-tuple-element.24), channel_id=1, source_target_pairs={{0,2},{1,3},{2,0},{3,1},{4,6},{5,7},{6,4},{7,5},{8,10},{9,11},{10,... | collective-permute-start | bytes 356360 | tf_op jit(solution)/shard_map/ppermute | solution.py:50
  7.3 5.7 %copy-start.14 = (bf16[464,128]{1,0:T(8,128)(2,1)S(1)}, bf16[464,128]{1,0:T(8,128)(2,1)}, u32[]{:S(2)}) copy-start(bf16[464,128]{1,0:T(8,128)(2,1)} %get-tuple-element.24) | copy-start | bytes 356356
  7.3 5.7 %copy-start.13 = (bf16[528,128]{1,0:T(8,128)(2,1)S(1)}, bf16[528,128]{1,0:T(8,128)(2,1)}, u32[]{:S(2)}) copy-start(bf16[528,128]{1,0:T(8,128)(2,1)} %get-tuple-element.25) | copy-start | bytes 405508
  7.3 58.2 %all-to-all-start = ((bf16[8,128,1536]{2,1,0:T(8,128)(2,1)}), bf16[8,128,1536]{2,1,0:T(8,128)(2,1)}, u32[]{:S(2)}, u32[]{:S(2)}) async-start(bf16[8,128,1536]{2,1,0:T(8,128)(2,1)} %broadcast_in_dim.4), calls=%async_computation | async-start | bytes 6291456 | tf_op jit(solution)/shard_map/all_to_all | solution.py:363
  13.0 13.4 %collective-permute-start.1 = (bf16[1456,128]{1,0:T(8,128)(2,1)S(1)}, bf16[1456,128]{1,0:T(8,128)(2,1)S(1)}, u32[]{:S(2)}, u32[]{:S(2)}) collective-permute-start(bf16[1456,128]{1,0:T(8,128)(2,1)S(1)} %pad_maximum_fusion.refs_0_), channel_id=1, source_target_pairs={{0,4},{1,5},{2,6},{3,7},{4,8},{5,9},{6,10},{7,11},{8,12},{9,13},{1... | collective-permute-start | bytes 1118216 | tf_op jit(solution)/shard_map/ppermute | solution.py:50
  14.8 11.7 %collective-permute-start.4 = (bf16[1456,128]{1,0:T(8,128)(2,1)S(1)}, bf16[1456,128]{1,0:T(8,128)(2,1)S(1)}, u32[]{:S(2)}, u32[]{:S(2)}) collective-permute-start(bf16[1456,128]{1,0:T(8,128)(2,1)S(1)} %pad_maximum_fusion.refs_0_), channel_id=1, source_target_pairs={{0,28},{1,29},{2,30},{3,31},{4,0},{5,1},{6,2},{7,3},{8,4},{9,5},{1... | collective-permute-start | bytes 1118216 | tf_op jit(solution)/shard_map/ppermute | solution.py:50
  26.4 9.6 %collective-permute-start.2 = (bf16[1456,128]{1,0:T(8,128)(2,1)S(1)}, bf16[1456,128]{1,0:T(8,128)(2,1)S(1)}, u32[]{:S(2)}, u32[]{:S(2)}) collective-permute-start(bf16[1456,128]{1,0:T(8,128)(2,1)S(1)} %collective-permute-done.1.refs_1_), channel_id=1, source_target_pairs={{0,4},{1,5},{2,6},{3,7},{4,8},{5,9},{6,10},{7,11},{8,12},{9,13},{1... | collective-permute-start | bytes 1118216 | tf_op jit(solution)/shard_map/ppermute | solution.py:50
  26.4 9.6 %collective-permute-start.5 = (bf16[1456,128]{1,0:T(8,128)(2,1)S(1)}, bf16[1456,128]{1,0:T(8,128)(2,1)S(1)}, u32[]{:S(2)}, u32[]{:S(2)}) collective-permute-start(bf16[1456,128]{1,0:T(8,128)(2,1)S(1)} %collective-permute-done.4.refs_4_), channel_id=1, source_target_pairs={{0,28},{1,29},{2,30},{3,31},{4,0},{5,1},{6,2},{7,3},{8,4},{9,5},{1... | collective-permute-start | bytes 1118216 | tf_op jit(solution)/shard_map/ppermute | solution.py:50
  36.0 8.8 %collective-permute-start.3 = (bf16[1456,128]{1,0:T(8,128)(2,1)S(1)}, bf16[1456,128]{1,0:T(8,128)(2,1)S(1)}, u32[]{:S(2)}, u32[]{:S(2)}) collective-permute-start(bf16[1456,128]{1,0:T(8,128)(2,1)S(1)} %collective-permute-done.2.refs_2_), channel_id=1, source_target_pairs={{0,4},{1,5},{2,6},{3,7},{4,8},{5,9},{6,10},{7,11},{8,12},{9,13},{1... | collective-permute-start | bytes 1118216 | tf_op jit(solution)/shard_map/ppermute | solution.py:50
  36.0 8.9 %collective-permute-start.6 = (bf16[1456,128]{1,0:T(8,128)(2,1)S(1)}, bf16[1456,128]{1,0:T(8,128)(2,1)S(1)}, u32[]{:S(2)}, u32[]{:S(2)}) collective-permute-start(bf16[1456,128]{1,0:T(8,128)(2,1)S(1)} %collective-permute-done.5.refs_5_), channel_id=1, source_target_pairs={{0,28},{1,29},{2,30},{3,31},{4,0},{5,1},{6,2},{7,3},{8,4},{9,5},{1... | collective-permute-start | bytes 1118216 | tf_op jit(solution)/shard_map/ppermute | solution.py:50
  44.8 6.2 %collective-permute-start.7 = (bf16[928,128]{1,0:T(8,128)(2,1)S(1)}, bf16[928,128]{1,0:T(8,128)(2,1)S(1)}, u32[]{:S(2)}, u32[]{:S(2)}) collective-permute-start(bf16[928,128]{1,0:T(8,128)(2,1)S(1)} %slice.16), channel_id=1, source_target_pairs={{0,4},{1,5},{2,6},{3,7},{4,8},{5,9},{6,10},{7,11},{8,12},{9,13},{1... | collective-permute-start | bytes 712712 | tf_op jit(solution)/shard_map/ppermute | solution.py:50
  44.9 4.7 %collective-permute-start.8 = (bf16[528,128]{1,0:T(8,128)(2,1)S(1)}, bf16[528,128]{1,0:T(8,128)(2,1)S(1)}, u32[]{:S(2)}, u32[]{:S(2)}) collective-permute-start(bf16[528,128]{1,0:T(8,128)(2,1)S(1)} %slice.17), channel_id=1, source_target_pairs={{0,28},{1,29},{2,30},{3,31},{4,0},{5,1},{6,2},{7,3},{8,4},{9,5},{1... | collective-permute-start | bytes 405512 | tf_op jit(solution)/shard_map/ppermute | solution.py:50
  52.8 1.0 copy-start.11
  53.9 10.7 %collective-permute-start.14 = (bf16[8,528,128]{2,1,0:T(8,128)(2,1)}, bf16[8,528,128]{2,1,0:T(8,128)(2,1)S(1)}, u32[]{:S(2)}, u32[]{:S(2)}) collective-permute-start(bf16[8,528,128]{2,1,0:T(8,128)(2,1)} %get-tuple-element.27.refs_5_), channel_id=1, source_target_pairs={{0,1},{1,0},{2,3},{3,2},{4,5},{5,4},{6,7},{7,6},{8,9},{9,8},{10,11... | collective-permute-start | bytes 3244040 | tf_op jit(solution)/shard_map/ppermute | solution.py:50
  58.6 4.0 %collective-permute-start.13 = (bf16[8,480,128]{2,1,0:T(8,128)(2,1)}, bf16[8,480,128]{2,1,0:T(8,128)(2,1)S(1)}, u32[]{:S(2)}, u32[]{:S(2)}) collective-permute-start(bf16[8,480,128]{2,1,0:T(8,128)(2,1)} %get-tuple-element.26.refs_0_), channel_id=1, source_target_pairs={{0,1},{1,0},{2,3},{3,2},{4,5},{5,4},{6,7},{7,6},{8,9},{9,8},{10,11... | collective-permute-start | bytes 2949128 | tf_op jit(solution)/shard_map/ppermute | solution.py:50
  59.2 24.3 %collective-permute-start.10 = (bf16[8,480,128]{2,1,0:T(8,128)(2,1)}, bf16[8,480,128]{2,1,0:T(8,128)(2,1)S(1)}, u32[]{:S(2)}, u32[]{:S(2)}) collective-permute-start(bf16[8,480,128]{2,1,0:T(8,128)(2,1)} %get-tuple-element.26.refs_0_), channel_id=1, source_target_pairs={{0,96},{1,97},{2,98},{3,99},{4,100},{5,101},{6,102},{7,103},{8,104... | collective-permute-start | bytes 2949128 | tf_op jit(solution)/shard_map/ppermute | solution.py:50
  61.7 23.7 %collective-permute-start.9 = (bf16[8,480,128]{2,1,0:T(8,128)(2,1)}, bf16[8,480,128]{2,1,0:T(8,128)(2,1)}, u32[]{:S(2)}, u32[]{:S(2)}) collective-permute-start(bf16[8,480,128]{2,1,0:T(8,128)(2,1)} %get-tuple-element.26.refs_0_), channel_id=1, source_target_pairs={{0,32},{1,33},{2,34},{3,35},{4,36},{5,37},{6,38},{7,39},{8,40},{9,... | collective-permute-start | bytes 2949128 | tf_op jit(solution)/shard_map/ppermute | solution.py:50
  61.8 24.8 %collective-permute-start.12 = (bf16[8,528,128]{2,1,0:T(8,128)(2,1)}, bf16[8,528,128]{2,1,0:T(8,128)(2,1)S(1)}, u32[]{:S(2)}, u32[]{:S(2)}) collective-permute-start(bf16[8,528,128]{2,1,0:T(8,128)(2,1)} %get-tuple-element.27.refs_5_), channel_id=1, source_target_pairs={{0,130},{1,131},{2,128},{3,129},{4,134},{5,135},{6,132},{7,133},{8... | collective-permute-start | bytes 3244040 | tf_op jit(solution)/shard_map/ppermute | solution.py:50
  62.5 1.0 copy-start.3
  63.5 25.3 %collective-permute-start.11 = (bf16[8,528,128]{2,1,0:T(8,128)(2,1)}, bf16[8,528,128]{2,1,0:T(8,128)(2,1)S(1)}, u32[]{:S(2)}, u32[]{:S(2)}) collective-permute-start(bf16[8,528,128]{2,1,0:T(8,128)(2,1)} %get-tuple-element.27.refs_5_), channel_id=1, source_target_pairs={{0,128},{1,129},{2,130},{3,131},{4,132},{5,133},{6,134},{7,135},{8... | collective-permute-start | bytes 3244040 | tf_op jit(solution)/shard_map/ppermute | solution.py:50
  64.5 1.0 copy-start.1
  65.5 13.5 %copy-start = (bf16[1,128,1536]{2,1,0:T(8,128)(2,1)S(1)}, bf16[1,128,1536]{2,1,0:T(8,128)(2,1)}, u32[]{:S(2)}) copy-start(bf16[1,128,1536]{2,1,0:T(8,128)(2,1)} %param.7) | copy-start | bytes 1179652
  65.5 1.3 copy-start.12
  73.6 0.7 copy-start.5
  74.3 21.6 %all-to-all-start.1 = ((bf16[8,160,128]{2,1,0:T(8,128)(2,1)}), bf16[8,160,128]{2,1,0:T(8,128)(2,1)}, u32[]{:S(2)}, u32[]{:S(2)}) async-start(bf16[8,160,128]{2,1,0:T(8,128)(2,1)} %copy-done.5), calls=%async_computation.1 | async-start | bytes 655360 | tf_op jit(solution)/shard_map/all_to_all | solution.py:398
  79.0 12.5 %collective-permute-start.16 = (bf16[16,1536]{1,0:T(8,128)(2,1)S(1)}, bf16[16,1536]{1,0:T(8,128)(2,1)S(1)}, u32[]{:S(2)}, u32[]{:S(2)}) collective-permute-start(bf16[16,1536]{1,0:T(8,128)(2,1)S(1)} %get-tuple-element.43), channel_id=1, source_target_pairs={{32,0},{64,32},{96,64},{128,96},{160,128},{192,160},{224,192},{33,... | collective-permute-start | bytes 147464 | tf_op jit(solution)/shard_map/ppermute | solution.py:400
  83.5 11.8 %collective-permute-start.15 = (bf16[16,1536]{1,0:T(8,128)(2,1)S(1)}, bf16[16,1536]{1,0:T(8,128)(2,1)S(1)}, u32[]{:S(2)}, u32[]{:S(2)}) collective-permute-start(bf16[16,1536]{1,0:T(8,128)(2,1)S(1)} %get-tuple-element.44), channel_id=1, source_target_pairs={{0,32},{32,64},{64,96},{96,128},{128,160},{160,192},{192,224},{1,3... | collective-permute-start | bytes 147464 | tf_op jit(solution)/shard_map/ppermute | solution.py:399
  91.5 0.6 copy-start.7
  95.3 0.6 copy-start.9
  95.9 24.5 %copy-start.2 = (bf16[8,528,128]{2,1,0:T(8,128)(2,1)S(1)}, bf16[8,528,128]{2,1,0:T(8,128)(2,1)}, u32[]{:S(2)}) copy-start(bf16[8,528,128]{2,1,0:T(8,128)(2,1)} %copy-done.1) | copy-start | bytes 3244036
  95.9 24.5 %copy-start.4 = (bf16[8,480,128]{2,1,0:T(8,128)(2,1)S(1)}, bf16[8,480,128]{2,1,0:T(8,128)(2,1)}, u32[]{:S(2)}) copy-start(bf16[8,480,128]{2,1,0:T(8,128)(2,1)} %copy-done.3) | copy-start | bytes 2949124
  95.9 24.5 %copy-start.6 = (bf16[31,1536]{1,0:T(8,128)(2,1)S(1)}, bf16[31,1536]{1,0:T(8,128)(2,1)}, u32[]{:S(2)}) copy-start(bf16[31,1536]{1,0:T(8,128)(2,1)} %taps_in.1) | copy-start | bytes 285700
  95.9 24.5 %copy-start.8 = (bf16[16,1536]{1,0:T(8,128)(2,1)S(1)}, bf16[16,1536]{1,0:T(8,128)(2,1)}, u32[]{:S(2)}) copy-start(bf16[16,1536]{1,0:T(8,128)(2,1)} %copy-done.7) | copy-start | bytes 147460
  95.9 24.5 %copy-start.10 = (bf16[16,1536]{1,0:T(8,128)(2,1)S(1)}, bf16[16,1536]{1,0:T(8,128)(2,1)}, u32[]{:S(2)}) copy-start(bf16[16,1536]{1,0:T(8,128)(2,1)} %copy-done.9) | copy-start | bytes 147460
  97.2 12.6 %collective-permute-start.17 = (bf16[4,480,128]{2,1,0:T(8,128)(2,1)S(1)}, bf16[4,480,128]{2,1,0:T(8,128)(2,1)S(1)}, u32[]{:S(2)}, u32[]{:S(2)}) collective-permute-start(bf16[4,480,128]{2,1,0:T(8,128)(2,1)S(1)} %get-tuple-element.39), channel_id=1, source_target_pairs={{0,96},{1,97},{2,98},{3,99},{4,100},{5,101},{6,102},{7,103},{8,104... | collective-permute-start | bytes 1474568 | tf_op jit(solution)/shard_map/ppermute | solution.py:50
  97.3 14.8 %collective-permute-start.19 = (bf16[4,528,128]{2,1,0:T(8,128)(2,1)S(1)}, bf16[4,528,128]{2,1,0:T(8,128)(2,1)S(1)}, u32[]{:S(2)}, u32[]{:S(2)}) collective-permute-start(bf16[4,528,128]{2,1,0:T(8,128)(2,1)S(1)} %get-tuple-element.41), channel_id=1, source_target_pairs={{0,130},{1,131},{2,128},{3,129},{4,134},{5,135},{6,132},{7,133},{8... | collective-permute-start | bytes 1622024 | tf_op jit(solution)/shard_map/ppermute | solution.py:50
  98.0 14.1 %collective-permute-start.18 = (bf16[4,480,128]{2,1,0:T(8,128)(2,1)S(1)}, bf16[4,480,128]{2,1,0:T(8,128)(2,1)S(1)}, u32[]{:S(2)}, u32[]{:S(2)}) collective-permute-start(bf16[4,480,128]{2,1,0:T(8,128)(2,1)S(1)} %get-tuple-element.40), channel_id=1, source_target_pairs={{0,32},{1,33},{2,34},{3,35},{4,36},{5,37},{6,38},{7,39},{8,40},{9,... | collective-permute-start | bytes 1474568 | tf_op jit(solution)/shard_map/ppermute | solution.py:50
  98.0 14.6 %collective-permute-start.20 = (bf16[4,528,128]{2,1,0:T(8,128)(2,1)S(1)}, bf16[4,528,128]{2,1,0:T(8,128)(2,1)S(1)}, u32[]{:S(2)}, u32[]{:S(2)}) collective-permute-start(bf16[4,528,128]{2,1,0:T(8,128)(2,1)S(1)} %get-tuple-element.42), channel_id=1, source_target_pairs={{0,128},{1,129},{2,130},{3,131},{4,132},{5,133},{6,134},{7,135},{8... | collective-permute-start | bytes 1622024 | tf_op jit(solution)/shard_map/ppermute | solution.py:50
  99.0 13.7 %collective-permute-start.21 = (bf16[8,480,128]{2,1,0:T(8,128)(2,1)}, bf16[8,480,128]{2,1,0:T(8,128)(2,1)S(1)}, u32[]{:S(2)}, u32[]{:S(2)}) collective-permute-start(bf16[8,480,128]{2,1,0:T(8,128)(2,1)} %collective-permute-done.9.beta_1.refs_1_), channel_id=1, source_target_pairs={{0,1},{1,0},{2,3},{3,2},{4,5},{5,4},{6,7},{7,6},{8,9},{9,8},{10,11... | collective-permute-start | bytes 2949128 | tf_op jit(solution)/shard_map/ppermute | solution.py:50
  109.8 4.5 %collective-permute-start.24 = (bf16[8,480,128]{2,1,0:T(8,128)(2,1)S(1)}, bf16[8,480,128]{2,1,0:T(8,128)(2,1)S(1)}, u32[]{:S(2)}, u32[]{:S(2)}) collective-permute-start(bf16[8,480,128]{2,1,0:T(8,128)(2,1)S(1)} %collective-permute-done.10.beta_3.refs_4_), channel_id=1, source_target_pairs={{0,1},{1,0},{2,3},{3,2},{4,5},{5,4},{6,7},{7,6},{8,9},{9,8},{10,11... | collective-permute-start | bytes 2949128 | tf_op jit(solution)/shard_map/ppermute | solution.py:50
  112.1 8.2 %collective-permute-start.25 = (bf16[8,528,128]{2,1,0:T(8,128)(2,1)S(1)}, bf16[8,528,128]{2,1,0:T(8,128)(2,1)S(1)}, u32[]{:S(2)}, u32[]{:S(2)}) collective-permute-start(bf16[8,528,128]{2,1,0:T(8,128)(2,1)S(1)} %collective-permute-done.11.gamma_1.refs_6_), channel_id=1, source_target_pairs={{0,1},{1,0},{2,3},{3,2},{4,5},{5,4},{6,7},{7,6},{8,9},{9,8},{10,11... | collective-permute-start | bytes 3244040 | tf_op jit(solution)/shard_map/ppermute | solution.py:50
  112.1 8.2 %collective-permute-start.28 = (bf16[8,528,128]{2,1,0:T(8,128)(2,1)S(1)}, bf16[8,528,128]{2,1,0:T(8,128)(2,1)S(1)}, u32[]{:S(2)}, u32[]{:S(2)}) collective-permute-start(bf16[8,528,128]{2,1,0:T(8,128)(2,1)S(1)} %collective-permute-done.12.gamma_3.refs_9_), channel_id=1, source_target_pairs={{0,1},{1,0},{2,3},{3,2},{4,5},{5,4},{6,7},{7,6},{8,9},{9,8},{10,11... | collective-permute-start | bytes 3244040 | tf_op jit(solution)/shard_map/ppermute | solution.py:50
  112.6 5.5 %collective-permute-start.22 = (bf16[4,480,128]{2,1,0:T(8,128)(2,1)S(1)}, bf16[4,480,128]{2,1,0:T(8,128)(2,1)S(1)}, u32[]{:S(2)}, u32[]{:S(2)}) collective-permute-start(bf16[4,480,128]{2,1,0:T(8,128)(2,1)S(1)} %collective-permute-done.17.refs_2_), channel_id=1, source_target_pairs={{0,1},{1,0},{2,3},{3,2},{4,5},{5,4},{6,7},{7,6},{8,9},{9,8},{10,11... | collective-permute-start | bytes 1474568 | tf_op jit(solution)/shard_map/ppermute | solution.py:50
  112.7 7.6 %collective-permute-start.26 = (bf16[4,528,128]{2,1,0:T(8,128)(2,1)S(1)}, bf16[4,528,128]{2,1,0:T(8,128)(2,1)S(1)}, u32[]{:S(2)}, u32[]{:S(2)}) collective-permute-start(bf16[4,528,128]{2,1,0:T(8,128)(2,1)S(1)} %collective-permute-done.19.refs_7_), channel_id=1, source_target_pairs={{0,1},{1,0},{2,3},{3,2},{4,5},{5,4},{6,7},{7,6},{8,9},{9,8},{10,11... | collective-permute-start | bytes 1622024 | tf_op jit(solution)/shard_map/ppermute | solution.py:50
  114.3 6.1 %collective-permute-start.27 = (bf16[4,528,128]{2,1,0:T(8,128)(2,1)S(1)}, bf16[4,528,128]{2,1,0:T(8,128)(2,1)S(1)}, u32[]{:S(2)}, u32[]{:S(2)}) collective-permute-start(bf16[4,528,128]{2,1,0:T(8,128)(2,1)S(1)} %collective-permute-done.20.refs_8_), channel_id=1, source_target_pairs={{0,1},{1,0},{2,3},{3,2},{4,5},{5,4},{6,7},{7,6},{8,9},{9,8},{10,11... | collective-permute-start | bytes 1622024 | tf_op jit(solution)/shard_map/ppermute | solution.py:50
  118.1 2.2 %collective-permute-start.23 = (bf16[4,480,128]{2,1,0:T(8,128)(2,1)S(1)}, bf16[4,480,128]{2,1,0:T(8,128)(2,1)S(1)}, u32[]{:S(2)}, u32[]{:S(2)}) collective-permute-start(bf16[4,480,128]{2,1,0:T(8,128)(2,1)S(1)} %collective-permute-done.18.refs_3_), channel_id=1, source_target_pairs={{0,1},{1,0},{2,3},{3,2},{4,5},{5,4},{6,7},{7,6},{8,9},{9,8},{10,11... | collective-permute-start | bytes 1474568 | tf_op jit(solution)/shard_map/ppermute | solution.py:50

commit v3 on v2

--- a/solution.py
+++ b/solution.py
@@ -99,7 +99,7 @@
 NEAR = BETA // 2 + 224
 
 
-def pack_kernel(x, w_qkv, w_out, w_glu, w_conv, beta, gam, normed, held, head, rows, sems):
+def pack_kernel(x, w_qkv, w_out, w_glu, w_conv, beta, gam, every, held, head, rows, sems, send_sems):
     ctx, y, a, _, _, core = whereabouts()
     glu, conv = core * 12, core * 6
     copies = [
@@ -119,6 +119,8 @@
     wait = run_copies(copies, sems)
     beta[432:464, :] = jnp.zeros((32, LANES), BF16)
     wait()
+    rows[...] = norm_rows(rows[...].astype(F32)).astype(BF16)
+    sent = run_copies([(rows, every.at[i]) for i in range(8)], send_sems)
     for j in range(HEADS):
 
         @pl.when(ctx == j)
@@ -131,7 +133,7 @@
     beta[336:432, :] = head[:, 128:256]
     for g in range(3):
         beta[432:464, 32 * g : 32 * (g + 1)] = head[32 * g : 32 * (g + 1), 256:288]
-    normed[...] = norm_rows(rows[...].astype(F32)).astype(BF16)
+    sent()
 
 
 STEPS = (0, -1, -2, -3, 1, 2, 3)
@@ -348,19 +350,19 @@
 
 def per_device(frames, lengths, w_qkv, w_out, w_glu, depth_kernel, w_conv_out):
     frame_rows = frames[0]
-    near, gamma, normed = pl.pallas_call(
+    near, gamma, own_frames = pl.pallas_call(
         pack_kernel,
-        out_shape=(shape(NEAR, LANES), shape(GAMMA, LANES), shape(ROWS, D)),
+        out_shape=(shape(NEAR, LANES), shape(GAMMA, LANES), shape(8, ROWS, D)),
         in_specs=[ANY] * 5,
-        out_specs=(VM,) * 3,
+        out_specs=(VM, VM, ANY),
         scratch_shapes=[
             pltpu.VMEM((96, 2304), BF16), pltpu.VMEM((96, 384), BF16), pltpu.VMEM((ROWS, D), BF16),
-            pltpu.SemaphoreType.DMA((14,)),
+            pltpu.SemaphoreType.DMA((14,)), pltpu.SemaphoreType.DMA((8,)),
         ],
         compiler_params=params(),
     )(frame_rows, w_qkv, w_out, w_glu, w_conv_out)
     far = send(near, SWAP_H)
-    every = lax.all_to_all(jnp.broadcast_to(normed[None], (8, ROWS, D)), "ctx", 0, 0)
+    every = lax.all_to_all(own_frames, "ctx", 0, 0)
 
     _, _, _, _, h, _ = whereabouts()
     pack = jnp.concatenate([jnp.where(h == 0, near, far), jnp.where(h == 0, far, near), gamma], axis=0)

time: 135 us -> 133 us (0.985)
  local copies, waits for them, and re-layouts: 9.29 us -> 6.35 us
  Pallas kernels: 25.7 us -> 27.2 us
    broadcast_in_dim x1 -> x0, local copies, waits for them, and re-layouts: 2.93 us -> none  [per_device(): jnp.broadcast_to(normed[None], (8, ROWS, D))]
    pallas_call x1, Pallas kernels: 2.44 us -> 3.99 us  [per_device(): pl.pallas_call(pack_kernel, out_shape=(shape(NEAR, LANES), shape(GAMMA, L...]
  transfers between devices with their start and end apart: 31 -> 31, of which waited for: 15 -> 15; matrix products, arithmetic and copies ran while one was open for 2% -> 0% of each run, Pallas kernels for 6% -> 6%
where the time goes in v3:
time: 133 us
  waiting for transfers between devices  49.3 us (37%)
  starting transfers between devices  48.7 us (37%)
  Pallas kernels  27.2 us (20%)
  local copies, waits for them, and re-layouts  6.35 us (5%)
    ppermute x27, waiting for transfers between devices, send(): return lax.ppermute(value, AXES, moves)  43.4 us
    ppermute x27, starting transfers between devices, send(): return lax.ppermute(value, AXES, moves)  32.2 us
    pallas_call x1, Pallas kernels, per_device(): pl.pallas_call(middle_kernel, out_shape=shape(ROWS, D), in_specs=[SM] + [...  13.5 us
    pallas_call x1, Pallas kernels, per_device(): pl.pallas_call(attend_kernel, out_shape=shape(8, WIDE, LANES), in_specs=[...  6.75 us
    unnamed x30, local copies, waits for them, and re-layouts  6.32 us
    all_to_all x1, starting transfers between devices, per_device(): every = lax.all_to_all(own_frames, 'ctx', 0, 0)  5.64 us
    all_to_all x1, starting transfers between devices, per_device(): att = lax.all_to_all(att, 'ctx', 0, 0)  4.65 us
    ppermute x1, starting transfers between devices, per_device(): frames_behind = lax.ppermute(halo[:HALO], 'ctx', down)  4.3 us
  transfers between devices with their start and end apart: 31, of which 15 were waited for; matrix products, arithmetic and copies ran while one was open for 0% of the time, Pallas kernels for 6%

profile of v3, /device:TPU:3, one launch (start us, length us, event | category | flops | bytes accessed | tf_op | source)
XLA Modules:
  0.0 132.7 jit_solution(14596757704487060039)
XLA Ops:
  0.0 4.0 %shard_map.73 = (bf16[464,128]{1,0:T(8,128)(2,1)}, bf16[528,128]{1,0:T(8,128)(2,1)}, bf16[8,128,1536]{2,1,0:T(8,128)(2,1)}) custom-call(bf16[128,1536]{1,0:T(8,128)(2,1)} %bitcast.2, bf16[96,2304]{1,0:T(8,128)(2,1)} %w_qkv.1, bf16[48,1536]{1,0:T(8,128)(2,1)} %w_out.1, bf16[96,3072]{1,0:T(8,128)(2,1)} %w_glu.1, bf16[96,1536]{1,0:T(8,128)(2,1)} %w_conv.1), custom_call_target="tpu_custom_call" | custom-call | tf_op jit(solution)/shard_map/pallas_call | solution.py:353
  4.0 1.9 %collective-permute-start = (bf16[464,128]{1,0:T(8,128)(2,1)}, bf16[464,128]{1,0:T(8,128)(2,1)S(1)}, u32[]{:S(2)}, u32[]{:S(2)}) collective-permute-start(bf16[464,128]{1,0:T(8,128)(2,1)} %get-tuple-element.24), channel_id=1, source_target_pairs={{0,2},{1,3},{2,0},{3,1},{4,6},{5,7},{6,4},{7,5},{8,10},{9,11},{10,... | collective-permute-start | bytes 356360 | tf_op jit(solution)/shard_map/ppermute | solution.py:50
  5.9 5.6 %all-to-all-start = ((bf16[8,128,1536]{2,1,0:T(8,128)(2,1)}), bf16[8,128,1536]{2,1,0:T(8,128)(2,1)}, u32[]{:S(2)}, u32[]{:S(2)}) async-start(bf16[8,128,1536]{2,1,0:T(8,128)(2,1)} %get-tuple-element.28), calls=%async_computation | async-start | bytes 6291456 | tf_op jit(solution)/shard_map/all_to_all | solution.py:365
  11.7 1.7 %collective-permute-start.1 = (bf16[1456,128]{1,0:T(8,128)(2,1)S(1)}, bf16[1456,128]{1,0:T(8,128)(2,1)S(1)}, u32[]{:S(2)}, u32[]{:S(2)}) collective-permute-start(bf16[1456,128]{1,0:T(8,128)(2,1)S(1)} %pad_maximum_fusion.refs_0_), channel_id=1, source_target_pairs={{0,4},{1,5},{2,6},{3,7},{4,8},{5,9},{6,10},{7,11},{8,12},{9,13},{1... | collective-permute-start | bytes 1118216 | tf_op jit(solution)/shard_map/ppermute | solution.py:50
  13.4 4.0 %collective-permute-start.4 = (bf16[1456,128]{1,0:T(8,128)(2,1)S(1)}, bf16[1456,128]{1,0:T(8,128)(2,1)S(1)}, u32[]{:S(2)}, u32[]{:S(2)}) collective-permute-start(bf16[1456,128]{1,0:T(8,128)(2,1)S(1)} %pad_maximum_fusion.refs_0_), channel_id=1, source_target_pairs={{0,28},{1,29},{2,30},{3,31},{4,0},{5,1},{6,2},{7,3},{8,4},{9,5},{1... | collective-permute-start | bytes 1118216 | tf_op jit(solution)/shard_map/ppermute | solution.py:50
  17.4 7.6 %collective-permute-done.1.refs_1_ = bf16[1456,128]{1,0:T(8,128)(2,1)S(1)} collective-permute-done((bf16[1456,128]{1,0:T(8,128)(2,1)S(1)}, bf16[1456,128]{1,0:T(8,128)(2,1)S(1)}, u32[]{:S(2)}, u32[]{:S(2)}) %collective-permute-start.1) | collective-permute-done | bytes 372768 | tf_op jit(solution)/shard_map/ppermute | solution.py:50
  25.0 2.7 %collective-permute-start.5 = (bf16[1456,128]{1,0:T(8,128)(2,1)S(1)}, bf16[1456,128]{1,0:T(8,128)(2,1)S(1)}, u32[]{:S(2)}, u32[]{:S(2)}) collective-permute-start(bf16[1456,128]{1,0:T(8,128)(2,1)S(1)} %collective-permute-done.4.refs_4_), channel_id=1, source_target_pairs={{0,28},{1,29},{2,30},{3,31},{4,0},{5,1},{6,2},{7,3},{8,4},{9,5},{1... | collective-permute-start | bytes 1118216 | tf_op jit(solution)/shard_map/ppermute | solution.py:50
  27.7 6.9 %collective-permute-done.2.refs_2_ = bf16[1456,128]{1,0:T(8,128)(2,1)S(1)} collective-permute-done((bf16[1456,128]{1,0:T(8,128)(2,1)S(1)}, bf16[1456,128]{1,0:T(8,128)(2,1)S(1)}, u32[]{:S(2)}, u32[]{:S(2)}) %collective-permute-start.2) | collective-permute-done | bytes 372768 | tf_op jit(solution)/shard_map/ppermute | solution.py:50
  34.6 2.7 %collective-permute-start.6 = (bf16[1456,128]{1,0:T(8,128)(2,1)S(1)}, bf16[1456,128]{1,0:T(8,128)(2,1)S(1)}, u32[]{:S(2)}, u32[]{:S(2)}) collective-permute-start(bf16[1456,128]{1,0:T(8,128)(2,1)S(1)} %collective-permute-done.5.refs_5_), channel_id=1, source_target_pairs={{0,28},{1,29},{2,30},{3,31},{4,0},{5,1},{6,2},{7,3},{8,4},{9,5},{1... | collective-permute-start | bytes 1118216 | tf_op jit(solution)/shard_map/ppermute | solution.py:50
  37.3 6.1 %collective-permute-done.3.refs_3_ = bf16[1456,128]{1,0:T(8,128)(2,1)S(1)} collective-permute-done((bf16[1456,128]{1,0:T(8,128)(2,1)S(1)}, bf16[1456,128]{1,0:T(8,128)(2,1)S(1)}, u32[]{:S(2)}, u32[]{:S(2)}) %collective-permute-start.3) | collective-permute-done | bytes 372768 | tf_op jit(solution)/shard_map/ppermute | solution.py:50
  43.5 2.7 %collective-permute-start.8 = (bf16[528,128]{1,0:T(8,128)(2,1)S(1)}, bf16[528,128]{1,0:T(8,128)(2,1)S(1)}, u32[]{:S(2)}, u32[]{:S(2)}) collective-permute-start(bf16[528,128]{1,0:T(8,128)(2,1)S(1)} %slice.17), channel_id=1, source_target_pairs={{0,28},{1,29},{2,30},{3,31},{4,0},{5,1},{6,2},{7,3},{8,4},{9,5},{1... | collective-permute-start | bytes 405512 | tf_op jit(solution)/shard_map/ppermute | solution.py:50
  46.2 2.0 %collective-permute-done.8.refs_8_ = bf16[528,128]{1,0:T(8,128)(2,1)S(1)} collective-permute-done((bf16[528,128]{1,0:T(8,128)(2,1)S(1)}, bf16[528,128]{1,0:T(8,128)(2,1)S(1)}, u32[]{:S(2)}, u32[]{:S(2)}) %collective-permute-start.8) | collective-permute-done | bytes 135200 | tf_op jit(solution)/shard_map/ppermute | solution.py:50
  48.2 1.4 %collective-permute-done.7.refs_7_ = bf16[928,128]{1,0:T(8,128)(2,1)S(1)} collective-permute-done((bf16[928,128]{1,0:T(8,128)(2,1)S(1)}, bf16[928,128]{1,0:T(8,128)(2,1)S(1)}, u32[]{:S(2)}, u32[]{:S(2)}) %collective-permute-start.7) | collective-permute-done | bytes 237600 | tf_op jit(solution)/shard_map/ppermute | solution.py:50
  49.6 1.8 %shard_map.74 = (bf16[8,2,96,384]{3,2,1,0:T(8,128)(2,1)S(1)}, bf16[8,480,128]{2,1,0:T(8,128)(2,1)}, bf16[8,528,128]{2,1,0:T(8,128)(2,1)}) custom-call(bf16[1456,128]{1,0:T(8,128)(2,1)S(1)} %pad_maximum_fusion.refs_0_, bf16[1456,128]{1,0:T(8,128)(2,1)S(1)} %collective-permute-done.1.refs_1_, bf16[1456,128]{1,0:T(8,128)(2,1)S(1)} %collective-permute-done.2.refs_2_, ...), custom_call_target="tpu_custom_call" | custom-call | tf_op jit(solution)/shard_map/pallas_call | solution.py:370
  51.4 1.0 copy-done.11
  52.5 4.7 %collective-permute-start.14 = (bf16[8,528,128]{2,1,0:T(8,128)(2,1)}, bf16[8,528,128]{2,1,0:T(8,128)(2,1)S(1)}, u32[]{:S(2)}, u32[]{:S(2)}) collective-permute-start(bf16[8,528,128]{2,1,0:T(8,128)(2,1)} %get-tuple-element.27.refs_5_), channel_id=1, source_target_pairs={{0,1},{1,0},{2,3},{3,2},{4,5},{5,4},{6,7},{7,6},{8,9},{9,8},{10,11... | collective-permute-start | bytes 3244040 | tf_op jit(solution)/shard_map/ppermute | solution.py:50
  57.8 2.5 %collective-permute-start.10 = (bf16[8,480,128]{2,1,0:T(8,128)(2,1)}, bf16[8,480,128]{2,1,0:T(8,128)(2,1)S(1)}, u32[]{:S(2)}, u32[]{:S(2)}) collective-permute-start(bf16[8,480,128]{2,1,0:T(8,128)(2,1)} %get-tuple-element.26.refs_0_), channel_id=1, source_target_pairs={{0,96},{1,97},{2,98},{3,99},{4,100},{5,101},{6,102},{7,103},{8,104... | collective-permute-start | bytes 2949128 | tf_op jit(solution)/shard_map/ppermute | solution.py:50
  60.4 0.8 collective-permute-done.13.refs_10_
  61.1 1.0 copy-done.3
  62.1 1.0 collective-permute-start.11
  63.1 1.0 copy-done.1
  64.1 1.3 copy-done.12
  65.4 6.8 %shard_map.75 = bf16[8,160,128]{2,1,0:T(8,128)(2,1)S(1)} custom-call(s32[1]{0:T(128)S(6)} %copy.8.length, bf16[8,128,1536]{2,1,0:T(8,128)(2,1)} %all-to-all-done.x, bf16[8,2,96,384]{3,2,1,0:T(8,128)(2,1)S(1)} %copy-done.12), custom_call_target="tpu_custom_call" | custom-call | flops 20000000000 | bytes 1048576 | tf_op jit(solution)/shard_map/pallas_call | solution.py:382
  72.2 0.7 copy-done.5
  72.9 4.6 %all-to-all-start.1 = ((bf16[8,160,128]{2,1,0:T(8,128)(2,1)}), bf16[8,160,128]{2,1,0:T(8,128)(2,1)}, u32[]{:S(2)}, u32[]{:S(2)}) async-start(bf16[8,160,128]{2,1,0:T(8,128)(2,1)} %copy-done.5), calls=%async_computation.1 | async-start | bytes 655360 | tf_op jit(solution)/shard_map/all_to_all | solution.py:400
  77.6 4.3 %collective-permute-start.16 = (bf16[16,1536]{1,0:T(8,128)(2,1)S(1)}, bf16[16,1536]{1,0:T(8,128)(2,1)S(1)}, u32[]{:S(2)}, u32[]{:S(2)}) collective-permute-start(bf16[16,1536]{1,0:T(8,128)(2,1)S(1)} %get-tuple-element.43), channel_id=1, source_target_pairs={{32,0},{64,32},{96,64},{128,96},{160,128},{192,160},{224,192},{33,... | collective-permute-start | bytes 147464 | tf_op jit(solution)/shard_map/ppermute | solution.py:402
  81.9 0.2 collective-permute-done.10.beta_3.refs_4_
  82.1 1.9 %collective-permute-start.15 = (bf16[16,1536]{1,0:T(8,128)(2,1)S(1)}, bf16[16,1536]{1,0:T(8,128)(2,1)S(1)}, u32[]{:S(2)}, u32[]{:S(2)}) collective-permute-start(bf16[16,1536]{1,0:T(8,128)(2,1)S(1)} %get-tuple-element.44), channel_id=1, source_target_pairs={{0,32},{32,64},{64,96},{96,128},{128,160},{160,192},{192,224},{1,3... | collective-permute-start | bytes 147464 | tf_op jit(solution)/shard_map/ppermute | solution.py:401
  84.1 1.1 collective-permute-done.12.gamma_3.refs_9_
  85.1 2.3 %collective-permute-done.11.gamma_1.refs_6_ = bf16[8,528,128]{2,1,0:T(8,128)(2,1)S(1)} collective-permute-done((bf16[8,528,128]{2,1,0:T(8,128)(2,1)}, bf16[8,528,128]{2,1,0:T(8,128)(2,1)S(1)}, u32[]{:S(2)}, u32[]{:S(2)}) %collective-permute-start.11) | collective-permute-done | bytes 1081376 | tf_op jit(solution)/shard_map/ppermute | solution.py:50
  87.4 2.7 %collective-permute-done.16.behind_in = bf16[16,1536]{1,0:T(8,128)(2,1)S(1)} collective-permute-done((bf16[16,1536]{1,0:T(8,128)(2,1)S(1)}, bf16[16,1536]{1,0:T(8,128)(2,1)S(1)}, u32[]{:S(2)}, u32[]{:S(2)}) %collective-permute-start.16) | collective-permute-done | bytes 49184 | tf_op jit(solution)/shard_map/ppermute | solution.py:402
  90.1 0.6 copy-done.7
  90.7 3.2 %collective-permute-done.15.before_in = bf16[16,1536]{1,0:T(8,128)(2,1)S(1)} collective-permute-done((bf16[16,1536]{1,0:T(8,128)(2,1)S(1)}, bf16[16,1536]{1,0:T(8,128)(2,1)S(1)}, u32[]{:S(2)}, u32[]{:S(2)}) %collective-permute-start.15) | collective-permute-done | bytes 49184 | tf_op jit(solution)/shard_map/ppermute | solution.py:401
  93.9 0.6 copy-done.9
  94.6 1.2 shard_map.76
  95.9 0.7 collective-permute-start.19
  96.6 1.0 collective-permute-start.20
  97.6 2.1 %collective-permute-start.21 = (bf16[8,480,128]{2,1,0:T(8,128)(2,1)}, bf16[8,480,128]{2,1,0:T(8,128)(2,1)S(1)}, u32[]{:S(2)}, u32[]{:S(2)}) collective-permute-start(bf16[8,480,128]{2,1,0:T(8,128)(2,1)} %collective-permute-done.9.beta_1.refs_1_), channel_id=1, source_target_pairs={{0,1},{1,0},{2,3},{3,2},{4,5},{5,4},{6,7},{7,6},{8,9},{9,8},{10,11... | collective-permute-start | bytes 2949128 | tf_op jit(solution)/shard_map/ppermute | solution.py:50
  99.8 8.6 %collective-permute-done.17.refs_2_ = bf16[4,480,128]{2,1,0:T(8,128)(2,1)S(1)} collective-permute-done((bf16[4,480,128]{2,1,0:T(8,128)(2,1)S(1)}, bf16[4,480,128]{2,1,0:T(8,128)(2,1)S(1)}, u32[]{:S(2)}, u32[]{:S(2)}) %collective-permute-start.17) | collective-permute-done | bytes 491552 | tf_op jit(solution)/shard_map/ppermute | solution.py:50
  108.4 2.3 %collective-permute-start.24 = (bf16[8,480,128]{2,1,0:T(8,128)(2,1)S(1)}, bf16[8,480,128]{2,1,0:T(8,128)(2,1)S(1)}, u32[]{:S(2)}, u32[]{:S(2)}) collective-permute-start(bf16[8,480,128]{2,1,0:T(8,128)(2,1)S(1)} %collective-permute-done.10.beta_3.refs_4_), channel_id=1, source_target_pairs={{0,1},{1,0},{2,3},{3,2},{4,5},{5,4},{6,7},{7,6},{8,9},{9,8},{10,11... | collective-permute-start | bytes 2949128 | tf_op jit(solution)/shard_map/ppermute | solution.py:50
  110.7 0.5 collective-permute-start.28
  111.3 0.4 collective-permute-start.26
  111.8 1.2 collective-permute-done.24.refs_14_
  112.9 0.4 collective-permute-start.27
  113.3 3.4 %collective-permute-done.22.refs_12_ = bf16[4,480,128]{2,1,0:T(8,128)(2,1)S(1)} collective-permute-done((bf16[4,480,128]{2,1,0:T(8,128)(2,1)S(1)}, bf16[4,480,128]{2,1,0:T(8,128)(2,1)S(1)}, u32[]{:S(2)}, u32[]{:S(2)}) %collective-permute-start.22) | collective-permute-done | bytes 491552 | tf_op jit(solution)/shard_map/ppermute | solution.py:50
  116.7 0.4 collective-permute-start.23
  117.1 1.9 %collective-permute-done.23.refs_13_ = bf16[4,480,128]{2,1,0:T(8,128)(2,1)S(1)} collective-permute-done((bf16[4,480,128]{2,1,0:T(8,128)(2,1)S(1)}, bf16[4,480,128]{2,1,0:T(8,128)(2,1)S(1)}, u32[]{:S(2)}, u32[]{:S(2)}) %collective-permute-start.23) | collective-permute-done | bytes 491552 | tf_op jit(solution)/shard_map/ppermute | solution.py:50
  119.0 13.5 %shard_map.77 = bf16[128,1536]{1,0:T(8,128)(2,1)} custom-call(s32[1]{0:T(128)S(6)} %copy.8.length, bf16[8,160,128]{2,1,0:T(8,128)(2,1)} %all-to-all-done.1.att_in, bf16[128,1536]{1,0:T(8,128)(2,1)S(1)} %bitcast.4, bf16[16,1536]{1,0:T(8,128)(2,1)S(1)} %copy-done.10, bf16[16,1536]{1,0:T(8,128)(2,1)S(1)} %copy-done.8, bf16[31,1536]{1,0:T(8,128)(2,1)S(1)} %copy-done.6, ...), custom_call_target="tpu_custom_call" | custom-call | tf_op jit(solution)/shard_map/pallas_call | solution.py:425
  (54 shorter events, 0.5 us)
Async XLA Ops:
  4.0 7.6 %collective-permute-start = (bf16[464,128]{1,0:T(8,128)(2,1)}, bf16[464,128]{1,0:T(8,128)(2,1)S(1)}, u32[]{:S(2)}, u32[]{:S(2)}) collective-permute-start(bf16[464,128]{1,0:T(8,128)(2,1)} %get-tuple-element.24), channel_id=1, source_target_pairs={{0,2},{1,3},{2,0},{3,1},{4,6},{5,7},{6,4},{7,5},{8,10},{9,11},{10,... | collective-permute-start | bytes 356360 | tf_op jit(solution)/shard_map/ppermute | solution.py:50
  5.9 5.6 %copy-start.14 = (bf16[464,128]{1,0:T(8,128)(2,1)S(1)}, bf16[464,128]{1,0:T(8,128)(2,1)}, u32[]{:S(2)}) copy-start(bf16[464,128]{1,0:T(8,128)(2,1)} %get-tuple-element.24) | copy-start | bytes 356356
  5.9 5.7 %copy-start.13 = (bf16[528,128]{1,0:T(8,128)(2,1)S(1)}, bf16[528,128]{1,0:T(8,128)(2,1)}, u32[]{:S(2)}) copy-start(bf16[528,128]{1,0:T(8,128)(2,1)} %get-tuple-element.25) | copy-start | bytes 405508
  5.9 58.2 %all-to-all-start = ((bf16[8,128,1536]{2,1,0:T(8,128)(2,1)}), bf16[8,128,1536]{2,1,0:T(8,128)(2,1)}, u32[]{:S(2)}, u32[]{:S(2)}) async-start(bf16[8,128,1536]{2,1,0:T(8,128)(2,1)} %get-tuple-element.28), calls=%async_computation | async-start | bytes 6291456 | tf_op jit(solution)/shard_map/all_to_all | solution.py:365
  11.7 13.4 %collective-permute-start.1 = (bf16[1456,128]{1,0:T(8,128)(2,1)S(1)}, bf16[1456,128]{1,0:T(8,128)(2,1)S(1)}, u32[]{:S(2)}, u32[]{:S(2)}) collective-permute-start(bf16[1456,128]{1,0:T(8,128)(2,1)S(1)} %pad_maximum_fusion.refs_0_), channel_id=1, source_target_pairs={{0,4},{1,5},{2,6},{3,7},{4,8},{5,9},{6,10},{7,11},{8,12},{9,13},{1... | collective-permute-start | bytes 1118216 | tf_op jit(solution)/shard_map/ppermute | solution.py:50
  13.4 11.7 %collective-permute-start.4 = (bf16[1456,128]{1,0:T(8,128)(2,1)S(1)}, bf16[1456,128]{1,0:T(8,128)(2,1)S(1)}, u32[]{:S(2)}, u32[]{:S(2)}) collective-permute-start(bf16[1456,128]{1,0:T(8,128)(2,1)S(1)} %pad_maximum_fusion.refs_0_), channel_id=1, source_target_pairs={{0,28},{1,29},{2,30},{3,31},{4,0},{5,1},{6,2},{7,3},{8,4},{9,5},{1... | collective-permute-start | bytes 1118216 | tf_op jit(solution)/shard_map/ppermute | solution.py:50
  25.0 9.6 %collective-permute-start.2 = (bf16[1456,128]{1,0:T(8,128)(2,1)S(1)}, bf16[1456,128]{1,0:T(8,128)(2,1)S(1)}, u32[]{:S(2)}, u32[]{:S(2)}) collective-permute-start(bf16[1456,128]{1,0:T(8,128)(2,1)S(1)} %collective-permute-done.1.refs_1_), channel_id=1, source_target_pairs={{0,4},{1,5},{2,6},{3,7},{4,8},{5,9},{6,10},{7,11},{8,12},{9,13},{1... | collective-permute-start | bytes 1118216 | tf_op jit(solution)/shard_map/ppermute | solution.py:50
  25.0 9.6 %collective-permute-start.5 = (bf16[1456,128]{1,0:T(8,128)(2,1)S(1)}, bf16[1456,128]{1,0:T(8,128)(2,1)S(1)}, u32[]{:S(2)}, u32[]{:S(2)}) collective-permute-start(bf16[1456,128]{1,0:T(8,128)(2,1)S(1)} %collective-permute-done.4.refs_4_), channel_id=1, source_target_pairs={{0,28},{1,29},{2,30},{3,31},{4,0},{5,1},{6,2},{7,3},{8,4},{9,5},{1... | collective-permute-start | bytes 1118216 | tf_op jit(solution)/shard_map/ppermute | solution.py:50
  34.6 8.8 %collective-permute-start.3 = (bf16[1456,128]{1,0:T(8,128)(2,1)S(1)}, bf16[1456,128]{1,0:T(8,128)(2,1)S(1)}, u32[]{:S(2)}, u32[]{:S(2)}) collective-permute-start(bf16[1456,128]{1,0:T(8,128)(2,1)S(1)} %collective-permute-done.2.refs_2_), channel_id=1, source_target_pairs={{0,4},{1,5},{2,6},{3,7},{4,8},{5,9},{6,10},{7,11},{8,12},{9,13},{1... | collective-permute-start | bytes 1118216 | tf_op jit(solution)/shard_map/ppermute | solution.py:50
  34.6 8.9 %collective-permute-start.6 = (bf16[1456,128]{1,0:T(8,128)(2,1)S(1)}, bf16[1456,128]{1,0:T(8,128)(2,1)S(1)}, u32[]{:S(2)}, u32[]{:S(2)}) collective-permute-start(bf16[1456,128]{1,0:T(8,128)(2,1)S(1)} %collective-permute-done.5.refs_5_), channel_id=1, source_target_pairs={{0,28},{1,29},{2,30},{3,31},{4,0},{5,1},{6,2},{7,3},{8,4},{9,5},{1... | collective-permute-start | bytes 1118216 | tf_op jit(solution)/shard_map/ppermute | solution.py:50
  43.4 6.2 %collective-permute-start.7 = (bf16[928,128]{1,0:T(8,128)(2,1)S(1)}, bf16[928,128]{1,0:T(8,128)(2,1)S(1)}, u32[]{:S(2)}, u32[]{:S(2)}) collective-permute-start(bf16[928,128]{1,0:T(8,128)(2,1)S(1)} %slice.16), channel_id=1, source_target_pairs={{0,4},{1,5},{2,6},{3,7},{4,8},{5,9},{6,10},{7,11},{8,12},{9,13},{1... | collective-permute-start | bytes 712712 | tf_op jit(solution)/shard_map/ppermute | solution.py:50
  43.5 4.7 %collective-permute-start.8 = (bf16[528,128]{1,0:T(8,128)(2,1)S(1)}, bf16[528,128]{1,0:T(8,128)(2,1)S(1)}, u32[]{:S(2)}, u32[]{:S(2)}) collective-permute-start(bf16[528,128]{1,0:T(8,128)(2,1)S(1)} %slice.17), channel_id=1, source_target_pairs={{0,28},{1,29},{2,30},{3,31},{4,0},{5,1},{6,2},{7,3},{8,4},{9,5},{1... | collective-permute-start | bytes 405512 | tf_op jit(solution)/shard_map/ppermute | solution.py:50
  51.4 1.0 copy-start.11
  52.5 10.7 %collective-permute-start.14 = (bf16[8,528,128]{2,1,0:T(8,128)(2,1)}, bf16[8,528,128]{2,1,0:T(8,128)(2,1)S(1)}, u32[]{:S(2)}, u32[]{:S(2)}) collective-permute-start(bf16[8,528,128]{2,1,0:T(8,128)(2,1)} %get-tuple-element.27.refs_5_), channel_id=1, source_target_pairs={{0,1},{1,0},{2,3},{3,2},{4,5},{5,4},{6,7},{7,6},{8,9},{9,8},{10,11... | collective-permute-start | bytes 3244040 | tf_op jit(solution)/shard_map/ppermute | solution.py:50
  57.2 4.0 %collective-permute-start.13 = (bf16[8,480,128]{2,1,0:T(8,128)(2,1)}, bf16[8,480,128]{2,1,0:T(8,128)(2,1)S(1)}, u32[]{:S(2)}, u32[]{:S(2)}) collective-permute-start(bf16[8,480,128]{2,1,0:T(8,128)(2,1)} %get-tuple-element.26.refs_0_), channel_id=1, source_target_pairs={{0,1},{1,0},{2,3},{3,2},{4,5},{5,4},{6,7},{7,6},{8,9},{9,8},{10,11... | collective-permute-start | bytes 2949128 | tf_op jit(solution)/shard_map/ppermute | solution.py:50
  57.8 24.3 %collective-permute-start.10 = (bf16[8,480,128]{2,1,0:T(8,128)(2,1)}, bf16[8,480,128]{2,1,0:T(8,128)(2,1)S(1)}, u32[]{:S(2)}, u32[]{:S(2)}) collective-permute-start(bf16[8,480,128]{2,1,0:T(8,128)(2,1)} %get-tuple-element.26.refs_0_), channel_id=1, source_target_pairs={{0,96},{1,97},{2,98},{3,99},{4,100},{5,101},{6,102},{7,103},{8,104... | collective-permute-start | bytes 2949128 | tf_op jit(solution)/shard_map/ppermute | solution.py:50
  60.3 23.7 %collective-permute-start.9 = (bf16[8,480,128]{2,1,0:T(8,128)(2,1)}, bf16[8,480,128]{2,1,0:T(8,128)(2,1)}, u32[]{:S(2)}, u32[]{:S(2)}) collective-permute-start(bf16[8,480,128]{2,1,0:T(8,128)(2,1)} %get-tuple-element.26.refs_0_), channel_id=1, source_target_pairs={{0,32},{1,33},{2,34},{3,35},{4,36},{5,37},{6,38},{7,39},{8,40},{9,... | collective-permute-start | bytes 2949128 | tf_op jit(solution)/shard_map/ppermute | solution.py:50
  60.3 24.8 %collective-permute-start.12 = (bf16[8,528,128]{2,1,0:T(8,128)(2,1)}, bf16[8,528,128]{2,1,0:T(8,128)(2,1)S(1)}, u32[]{:S(2)}, u32[]{:S(2)}) collective-permute-start(bf16[8,528,128]{2,1,0:T(8,128)(2,1)} %get-tuple-element.27.refs_5_), channel_id=1, source_target_pairs={{0,130},{1,131},{2,128},{3,129},{4,134},{5,135},{6,132},{7,133},{8... | collective-permute-start | bytes 3244040 | tf_op jit(solution)/shard_map/ppermute | solution.py:50
  61.1 1.0 copy-start.3
  62.1 25.3 %collective-permute-start.11 = (bf16[8,528,128]{2,1,0:T(8,128)(2,1)}, bf16[8,528,128]{2,1,0:T(8,128)(2,1)S(1)}, u32[]{:S(2)}, u32[]{:S(2)}) collective-permute-start(bf16[8,528,128]{2,1,0:T(8,128)(2,1)} %get-tuple-element.27.refs_5_), channel_id=1, source_target_pairs={{0,128},{1,129},{2,130},{3,131},{4,132},{5,133},{6,134},{7,135},{8... | collective-permute-start | bytes 3244040 | tf_op jit(solution)/shard_map/ppermute | solution.py:50
  63.1 1.0 copy-start.1
  64.1 13.5 %copy-start = (bf16[1,128,1536]{2,1,0:T(8,128)(2,1)S(1)}, bf16[1,128,1536]{2,1,0:T(8,128)(2,1)}, u32[]{:S(2)}) copy-start(bf16[1,128,1536]{2,1,0:T(8,128)(2,1)} %param.7) | copy-start | bytes 1179652
  64.1 1.3 copy-start.12
  72.2 0.7 copy-start.5
  72.9 21.6 %all-to-all-start.1 = ((bf16[8,160,128]{2,1,0:T(8,128)(2,1)}), bf16[8,160,128]{2,1,0:T(8,128)(2,1)}, u32[]{:S(2)}, u32[]{:S(2)}) async-start(bf16[8,160,128]{2,1,0:T(8,128)(2,1)} %copy-done.5), calls=%async_computation.1 | async-start | bytes 655360 | tf_op jit(solution)/shard_map/all_to_all | solution.py:400
  77.6 12.5 %collective-permute-start.16 = (bf16[16,1536]{1,0:T(8,128)(2,1)S(1)}, bf16[16,1536]{1,0:T(8,128)(2,1)S(1)}, u32[]{:S(2)}, u32[]{:S(2)}) collective-permute-start(bf16[16,1536]{1,0:T(8,128)(2,1)S(1)} %get-tuple-element.43), channel_id=1, source_target_pairs={{32,0},{64,32},{96,64},{128,96},{160,128},{192,160},{224,192},{33,... | collective-permute-start | bytes 147464 | tf_op jit(solution)/shard_map/ppermute | solution.py:402
  82.1 11.8 %collective-permute-start.15 = (bf16[16,1536]{1,0:T(8,128)(2,1)S(1)}, bf16[16,1536]{1,0:T(8,128)(2,1)S(1)}, u32[]{:S(2)}, u32[]{:S(2)}) collective-permute-start(bf16[16,1536]{1,0:T(8,128)(2,1)S(1)} %get-tuple-element.44), channel_id=1, source_target_pairs={{0,32},{32,64},{64,96},{96,128},{128,160},{160,192},{192,224},{1,3... | collective-permute-start | bytes 147464 | tf_op jit(solution)/shard_map/ppermute | solution.py:401
  90.1 0.6 copy-start.7
  93.9 0.6 copy-start.9
  94.5 24.5 %copy-start.2 = (bf16[8,528,128]{2,1,0:T(8,128)(2,1)S(1)}, bf16[8,528,128]{2,1,0:T(8,128)(2,1)}, u32[]{:S(2)}) copy-start(bf16[8,528,128]{2,1,0:T(8,128)(2,1)} %copy-done.1) | copy-start | bytes 3244036
  94.5 24.5 %copy-start.4 = (bf16[8,480,128]{2,1,0:T(8,128)(2,1)S(1)}, bf16[8,480,128]{2,1,0:T(8,128)(2,1)}, u32[]{:S(2)}) copy-start(bf16[8,480,128]{2,1,0:T(8,128)(2,1)} %copy-done.3) | copy-start | bytes 2949124
  94.5 24.5 %copy-start.6 = (bf16[31,1536]{1,0:T(8,128)(2,1)S(1)}, bf16[31,1536]{1,0:T(8,128)(2,1)}, u32[]{:S(2)}) copy-start(bf16[31,1536]{1,0:T(8,128)(2,1)} %taps_in.1) | copy-start | bytes 285700
  94.5 24.5 %copy-start.8 = (bf16[16,1536]{1,0:T(8,128)(2,1)S(1)}, bf16[16,1536]{1,0:T(8,128)(2,1)}, u32[]{:S(2)}) copy-start(bf16[16,1536]{1,0:T(8,128)(2,1)} %copy-done.7) | copy-start | bytes 147460
  94.5 24.5 %copy-start.10 = (bf16[16,1536]{1,0:T(8,128)(2,1)S(1)}, bf16[16,1536]{1,0:T(8,128)(2,1)}, u32[]{:S(2)}) copy-start(bf16[16,1536]{1,0:T(8,128)(2,1)} %copy-done.9) | copy-start | bytes 147460
  95.8 12.6 %collective-permute-start.17 = (bf16[4,480,128]{2,1,0:T(8,128)(2,1)S(1)}, bf16[4,480,128]{2,1,0:T(8,128)(2,1)S(1)}, u32[]{:S(2)}, u32[]{:S(2)}) collective-permute-start(bf16[4,480,128]{2,1,0:T(8,128)(2,1)S(1)} %get-tuple-element.39), channel_id=1, source_target_pairs={{0,96},{1,97},{2,98},{3,99},{4,100},{5,101},{6,102},{7,103},{8,104... | collective-permute-start | bytes 1474568 | tf_op jit(solution)/shard_map/ppermute | solution.py:50
  95.9 14.8 %collective-permute-start.19 = (bf16[4,528,128]{2,1,0:T(8,128)(2,1)S(1)}, bf16[4,528,128]{2,1,0:T(8,128)(2,1)S(1)}, u32[]{:S(2)}, u32[]{:S(2)}) collective-permute-start(bf16[4,528,128]{2,1,0:T(8,128)(2,1)S(1)} %get-tuple-element.41), channel_id=1, source_target_pairs={{0,130},{1,131},{2,128},{3,129},{4,134},{5,135},{6,132},{7,133},{8... | collective-permute-start | bytes 1622024 | tf_op jit(solution)/shard_map/ppermute | solution.py:50
  96.6 14.1 %collective-permute-start.18 = (bf16[4,480,128]{2,1,0:T(8,128)(2,1)S(1)}, bf16[4,480,128]{2,1,0:T(8,128)(2,1)S(1)}, u32[]{:S(2)}, u32[]{:S(2)}) collective-permute-start(bf16[4,480,128]{2,1,0:T(8,128)(2,1)S(1)} %get-tuple-element.40), channel_id=1, source_target_pairs={{0,32},{1,33},{2,34},{3,35},{4,36},{5,37},{6,38},{7,39},{8,40},{9,... | collective-permute-start | bytes 1474568 | tf_op jit(solution)/shard_map/ppermute | solution.py:50
  96.6 14.6 %collective-permute-start.20 = (bf16[4,528,128]{2,1,0:T(8,128)(2,1)S(1)}, bf16[4,528,128]{2,1,0:T(8,128)(2,1)S(1)}, u32[]{:S(2)}, u32[]{:S(2)}) collective-permute-start(bf16[4,528,128]{2,1,0:T(8,128)(2,1)S(1)} %get-tuple-element.42), channel_id=1, source_target_pairs={{0,128},{1,129},{2,130},{3,131},{4,132},{5,133},{6,134},{7,135},{8... | collective-permute-start | bytes 1622024 | tf_op jit(solution)/shard_map/ppermute | solution.py:50
  97.6 13.7 %collective-permute-start.21 = (bf16[8,480,128]{2,1,0:T(8,128)(2,1)}, bf16[8,480,128]{2,1,0:T(8,128)(2,1)S(1)}, u32[]{:S(2)}, u32[]{:S(2)}) collective-permute-start(bf16[8,480,128]{2,1,0:T(8,128)(2,1)} %collective-permute-done.9.beta_1.refs_1_), channel_id=1, source_target_pairs={{0,1},{1,0},{2,3},{3,2},{4,5},{5,4},{6,7},{7,6},{8,9},{9,8},{10,11... | collective-permute-start | bytes 2949128 | tf_op jit(solution)/shard_map/ppermute | solution.py:50
  108.4 4.5 %collective-permute-start.24 = (bf16[8,480,128]{2,1,0:T(8,128)(2,1)S(1)}, bf16[8,480,128]{2,1,0:T(8,128)(2,1)S(1)}, u32[]{:S(2)}, u32[]{:S(2)}) collective-permute-start(bf16[8,480,128]{2,1,0:T(8,128)(2,1)S(1)} %collective-permute-done.10.beta_3.refs_4_), channel_id=1, source_target_pairs={{0,1},{1,0},{2,3},{3,2},{4,5},{5,4},{6,7},{7,6},{8,9},{9,8},{10,11... | collective-permute-start | bytes 2949128 | tf_op jit(solution)/shard_map/ppermute | solution.py:50
  110.7 8.2 %collective-permute-start.25 = (bf16[8,528,128]{2,1,0:T(8,128)(2,1)S(1)}, bf16[8,528,128]{2,1,0:T(8,128)(2,1)S(1)}, u32[]{:S(2)}, u32[]{:S(2)}) collective-permute-start(bf16[8,528,128]{2,1,0:T(8,128)(2,1)S(1)} %collective-permute-done.11.gamma_1.refs_6_), channel_id=1, source_target_pairs={{0,1},{1,0},{2,3},{3,2},{4,5},{5,4},{6,7},{7,6},{8,9},{9,8},{10,11... | collective-permute-start | bytes 3244040 | tf_op jit(solution)/shard_map/ppermute | solution.py:50
  110.7 8.2 %collective-permute-start.28 = (bf16[8,528,128]{2,1,0:T(8,128)(2,1)S(1)}, bf16[8,528,128]{2,1,0:T(8,128)(2,1)S(1)}, u32[]{:S(2)}, u32[]{:S(2)}) collective-permute-start(bf16[8,528,128]{2,1,0:T(8,128)(2,1)S(1)} %collective-permute-done.12.gamma_3.refs_9_), channel_id=1, source_target_pairs={{0,1},{1,0},{2,3},{3,2},{4,5},{5,4},{6,7},{7,6},{8,9},{9,8},{10,11... | collective-permute-start | bytes 3244040 | tf_op jit(solution)/shard_map/ppermute | solution.py:50
  111.2 5.5 %collective-permute-start.22 = (bf16[4,480,128]{2,1,0:T(8,128)(2,1)S(1)}, bf16[4,480,128]{2,1,0:T(8,128)(2,1)S(1)}, u32[]{:S(2)}, u32[]{:S(2)}) collective-permute-start(bf16[4,480,128]{2,1,0:T(8,128)(2,1)S(1)} %collective-permute-done.17.refs_2_), channel_id=1, source_target_pairs={{0,1},{1,0},{2,3},{3,2},{4,5},{5,4},{6,7},{7,6},{8,9},{9,8},{10,11... | collective-permute-start | bytes 1474568 | tf_op jit(solution)/shard_map/ppermute | solution.py:50
  111.3 7.6 %collective-permute-start.26 = (bf16[4,528,128]{2,1,0:T(8,128)(2,1)S(1)}, bf16[4,528,128]{2,1,0:T(8,128)(2,1)S(1)}, u32[]{:S(2)}, u32[]{:S(2)}) collective-permute-start(bf16[4,528,128]{2,1,0:T(8,128)(2,1)S(1)} %collective-permute-done.19.refs_7_), channel_id=1, source_target_pairs={{0,1},{1,0},{2,3},{3,2},{4,5},{5,4},{6,7},{7,6},{8,9},{9,8},{10,11... | collective-permute-start | bytes 1622024 | tf_op jit(solution)/shard_map/ppermute | solution.py:50
  112.9 6.1 %collective-permute-start.27 = (bf16[4,528,128]{2,1,0:T(8,128)(2,1)S(1)}, bf16[4,528,128]{2,1,0:T(8,128)(2,1)S(1)}, u32[]{:S(2)}, u32[]{:S(2)}) collective-permute-start(bf16[4,528,128]{2,1,0:T(8,128)(2,1)S(1)} %collective-permute-done.20.refs_8_), channel_id=1, source_target_pairs={{0,1},{1,0},{2,3},{3,2},{4,5},{5,4},{6,7},{7,6},{8,9},{9,8},{10,11... | collective-permute-start | bytes 1622024 | tf_op jit(solution)/shard_map/ppermute | solution.py:50
  116.7 2.2 %collective-permute-start.23 = (bf16[4,480,128]{2,1,0:T(8,128)(2,1)S(1)}, bf16[4,480,128]{2,1,0:T(8,128)(2,1)S(1)}, u32[]{:S(2)}, u32[]{:S(2)}) collective-permute-start(bf16[4,480,128]{2,1,0:T(8,128)(2,1)S(1)} %collective-permute-done.18.refs_3_), channel_id=1, source_target_pairs={{0,1},{1,0},{2,3},{3,2},{4,5},{5,4},{6,7},{7,6},{8,9},{9,8},{10,11... | collective-permute-start | bytes 1474568 | tf_op jit(solution)/shard_map/ppermute | solution.py:50
